TPU v7x, 128 devices: a whole 4x4x4 slice. The times are simulated.
128 devices in a mesh: rep: 8 (over x_lo, z), tp: 16 (over y, x_hi, core).
Axes of the slice: x: 4 (x_hi: 2, x_lo: 2; x = x_hi * 2 + x_lo), y: 4, z: 4, core: 2. Of those that a mesh axis runs over, the one named last changes fastest.
Arguments:
- query_weight: bfloat16 [8192, 4096], P(('rep', 'tp')), may hold values from -0.0625 to 0.0625
- key_weight: bfloat16 [8192, 512], P(('rep', 'tp')), may hold values from -0.0625 to 0.0625
- value_weight: bfloat16 [8192, 512], P(('rep', 'tp')), may hold values from -0.0625 to 0.0625
- output_weight: bfloat16 [8192, 4096], P(('rep', 'tp')), may hold values from -0.375 to 0.375
- query_amax: float32 [4096], replicated, may hold values from 0.5 to 20
- key_amax: float32 [512], replicated, may hold values from 0.5 to 20
- hidden: bfloat16 [2560, 2, 8192], P('rep'), may hold values from -6 to 6
- positions: int32 [2560], P('rep'), may hold values from 0 to 2046
- cache_keys: bfloat16 [2560, 4, 256, 128], P(('rep', 'tp')), may hold values from -60 to 60
- cache_values: bfloat16 [2560, 4, 256, 128], P(('rep', 'tp')), may hold values from -6 to 6
- lengths: int32 [2560], P(('rep', 'tp')), may hold values from 1 to 256, as said below
Outputs:
- attn_out: bfloat16 [2560, 2, 8192], P('rep', None, 'tp')
Inputs may be any that keep to these rules, and one draw needn't show every extreme that they name: `lengths`: in each aligned block of 20 sequences the first has 256 live slots.
All inputs are finite; a program needn't handle non-finite values.
Results may differ from a plain program's by a relative error of at most 0.0095.
Values may be sent and summed in bfloat16 or wider, within the bound.
A program may use at most 128 MiB of HBM per device.

v0:
```python
import jax
import jax.numpy as jnp
from jax import lax
from jax.sharding import PartitionSpec as P

HQ = 32
KVH = 4
HD = 128


ROPE_THETA = 1000000.0


def smoothing(query_amax, key_amax):
    group_size = HQ // KVH
    half_width = HD // 2
    query_peak = jnp.max(query_amax.reshape(KVH, group_size, 2, half_width), axis=(1, 2))
    key_peak = jnp.max(key_amax.reshape(KVH, 2, half_width), axis=1)
    factor = jnp.sqrt(key_peak / query_peak)
    return jnp.concatenate([factor, factor], axis=1)


def rotary(vectors, angles):
    half_width = vectors.shape[-1] // 2
    first_half = vectors[..., :half_width]
    second = vectors[..., half_width:]
    cosine = jnp.cos(angles)
    sine_part = jnp.sin(angles)
    return jnp.concatenate(
        [first_half * cosine - second * sine_part, second * cosine + first_half * sine_part],
        axis=-1,
    )


def attend(queries, fresh_keys, fresh_values, cache_keys, cache_values, lengths):
    block_seqs = queries.shape[0]
    group_size = HQ // KVH
    score_scale = HD ** (-0.5)
    grouped = queries.reshape(block_seqs, 2, KVH, group_size, HD)
    cache_scores = (
        jnp.einsum("btghd,bgld->btghl", grouped, cache_keys, preferred_element_type=jnp.float32)
        * score_scale
    )
    fresh_scores = (
        jnp.einsum("btghd,bugd->btghu", grouped, fresh_keys, preferred_element_type=jnp.float32)
        * score_scale
    )
    slot_index = jnp.arange(cache_keys.shape[2], dtype=jnp.int32)
    live_slots = slot_index[None, :] < lengths[:, None]
    cache_scores = jnp.where(live_slots[:, None, None, None, :], cache_scores, -jnp.inf)
    token_index = jnp.arange(2, dtype=jnp.int32)
    earlier = token_index[None, :] <= token_index[:, None]
    fresh_scores = jnp.where(earlier[None, :, None, None, :], fresh_scores, -jnp.inf)
    row_max = jnp.maximum(jnp.max(cache_scores, axis=-1), jnp.max(fresh_scores, axis=-1))
    cache_probs = jnp.exp(cache_scores - row_max[..., None])
    fresh_probs = jnp.exp(fresh_scores - row_max[..., None])
    weight_sum = jnp.sum(cache_probs, axis=-1) + jnp.sum(fresh_probs, axis=-1)
    mixed_sum = jnp.einsum(
        "btghl,bgld->btghd",
        cache_probs.astype(jnp.bfloat16),
        cache_values,
        preferred_element_type=jnp.float32,
    )
    mixed_sum = mixed_sum + jnp.einsum(
        "btghu,bugd->btghd",
        fresh_probs.astype(jnp.bfloat16),
        fresh_values,
        preferred_element_type=jnp.float32,
    )
    return (mixed_sum / weight_sum[..., None]).astype(jnp.bfloat16).reshape(block_seqs, 2, HQ * HD)


def pair_split(matrix, tp_count):
    row_count = matrix.shape[0]
    duplicate = tp_count // KVH
    piece_width = HD // 2 // duplicate
    shaped = matrix.reshape(row_count, KVH, 2, duplicate, piece_width)
    return jnp.swapaxes(shaped, 2, 3).reshape(row_count, tp_count, 2 * piece_width)


def natural_order(pieces, duplicate):
    held_seqs = pieces.shape[0]
    piece_width = pieces.shape[-1] // 2
    shaped = pieces.reshape(held_seqs, KVH, duplicate, 2, 2, piece_width)
    return jnp.transpose(shaped, (0, 3, 1, 4, 2, 5)).reshape(held_seqs, 2, KVH, HD)


def bundle(query_weight, key_weight, value_weight, output_weight, tp_count):
    row_count = query_weight.shape[0]
    parts_list = [
        query_weight.reshape(row_count, tp_count, -1),
        pair_split(key_weight, tp_count),
        pair_split(value_weight, tp_count),
        output_weight.reshape(row_count, tp_count, -1),
    ]
    return jnp.concatenate(parts_list, axis=2).reshape(row_count, -1)


def body(
    query_weight,
    key_weight,
    value_weight,
    output_weight,
    query_amax,
    key_amax,
    hidden,
    positions,
    cache_keys,
    cache_values,
    lengths,
):
    tp_count = lax.axis_size("tp")
    rep_count = lax.axis_size("rep")
    tp_rank = lax.axis_index("tp")
    duplicate = tp_count // KVH
    piece_width = HD // 2 // duplicate
    q_width = HQ * HD // tp_count
    kv_width = KVH * HD // tp_count
    heads_here = HQ // tp_count
    split_at = q_width + 2 * kv_width
    factor = smoothing(query_amax, key_amax)
    packed = bundle(query_weight, key_weight, value_weight, output_weight, tp_count)
    shard_rows = packed.shape[0]
    group_rows = lax.all_gather(packed, "rep", axis=0, tiled=True)
    spread = lax.all_to_all(group_rows, "tp", split_axis=1, concat_axis=0, tiled=True)
    delivered = jnp.swapaxes(spread.reshape(tp_count, rep_count, shard_rows, -1), 0, 1).reshape(
        tp_count * rep_count * shard_rows, -1
    )
    model_width = delivered.shape[0]
    output_local = delivered[:, split_at:]
    group_size = HQ // KVH
    head_factor = lax.dynamic_slice_in_dim(
        jnp.repeat(factor, group_size, axis=0), tp_rank * heads_here, heads_here, 0
    )
    key_factor = lax.dynamic_slice_in_dim(
        pair_split(factor.reshape(1, KVH * HD), tp_count)[0], tp_rank, 1, 0
    )
    query_cols = (
        (
            delivered[:, :q_width].astype(jnp.float32).reshape(model_width, heads_here, HD)
            * head_factor[None]
        )
        .astype(jnp.bfloat16)
        .reshape(model_width, q_width)
    )
    key_cols = (delivered[:, q_width : q_width + kv_width].astype(jnp.float32) / key_factor).astype(
        jnp.bfloat16
    )
    projection = jnp.concatenate(
        [query_cols, key_cols, delivered[:, q_width + kv_width : split_at]], axis=1
    )
    seq_count = hidden.shape[0]
    flat_rows = hidden.reshape(seq_count * 2, model_width)
    projected = jnp.dot(flat_rows, projection, preferred_element_type=jnp.float32)
    token_place = positions[:, None] + jnp.arange(2, dtype=jnp.int32)[None, :]
    place_float = token_place.astype(jnp.float32)[:, :, None]
    query_index = jnp.arange(HD // 2, dtype=jnp.int32).astype(jnp.float32)
    query_freq = ROPE_THETA ** (-2.0 * query_index / HD)
    key_index = (
        tp_rank % duplicate * piece_width + jnp.arange(piece_width, dtype=jnp.int32)
    ).astype(jnp.float32)
    key_freq = ROPE_THETA ** (-2.0 * key_index / HD)
    query_rot = rotary(
        projected[:, :q_width].reshape(seq_count, 2, heads_here, HD),
        (place_float * query_freq)[:, :, None, :],
    ).astype(jnp.bfloat16)
    key_rot = rotary(
        projected[:, q_width : q_width + kv_width].reshape(seq_count, 2, kv_width),
        place_float * key_freq,
    ).astype(jnp.bfloat16)
    value_new = (
        projected[:, q_width + kv_width :].astype(jnp.bfloat16).reshape(seq_count, 2, kv_width)
    )
    outgoing = jnp.concatenate(
        [query_rot.reshape(seq_count, 2, q_width), key_rot, value_new], axis=2
    ).reshape(seq_count, 2 * split_at)
    arrived = lax.all_to_all(outgoing, "tp", split_axis=0, concat_axis=1, tiled=True)
    held_seqs = arrived.shape[0]
    arranged = arrived.reshape(held_seqs, tp_count, 2, split_at)
    query_all = jnp.transpose(
        arranged[..., :q_width].reshape(held_seqs, tp_count, 2, heads_here, HD), (0, 2, 1, 3, 4)
    ).reshape(held_seqs, 2, HQ, HD)
    key_all = natural_order(arranged[..., q_width : q_width + kv_width], duplicate)
    value_all = natural_order(arranged[..., q_width + kv_width :], duplicate)
    mixed_heads = attend(query_all, key_all, value_all, cache_keys, cache_values, lengths)
    gathered_heads = lax.all_to_all(mixed_heads, "tp", split_axis=2, concat_axis=0, tiled=True)
    head_rows = gathered_heads.reshape(seq_count * 2, q_width)
    summed = lax.psum_scatter(
        lax.dot_general(
            output_local, head_rows, (((1,), (1,)), ((), ())), preferred_element_type=jnp.float32
        ),
        "tp",
        scatter_dimension=0,
        tiled=True,
    )
    return jnp.transpose(summed).astype(jnp.bfloat16).reshape(seq_count, 2, -1)


def solution(mesh):
    in_specs = (
        P(("rep", "tp"), None),
        P(("rep", "tp"), None),
        P(("rep", "tp"), None),
        P(("rep", "tp"), None),
        P(),
        P(),
        P("rep", None, None),
        P("rep"),
        P(("rep", "tp"), None, None, None),
        P(("rep", "tp"), None, None, None),
        P(("rep", "tp")),
    )
    out_specs = P("rep", None, "tp")
    return jax.shard_map(body, mesh=mesh, in_specs=in_specs, out_specs=out_specs, check_vma=False)
```

profile of v0, /device:TPU:1, one launch (start us, length us, event | category | flops | bytes accessed | tf_op | source)
XLA Modules:
  0.0 535.5 jit_solution(15618577837946367477)
XLA Ops:
  11.9 2.0 reshape.179
  13.9 105.3 %all-gather.2.cloned.1.call-done = bf16[512,9216]{1,0:T(8,128)(2,1)} async-done(((bf16[64,9216]{1,0:T(8,128)(2,1)}), bf16[512,9216]{1,0:T(8,128)(2,1)}) %all-gather.2.cloned.1.call-update) | async-done | bytes 9437200 | tf_op jit(solution)/shard_map/all_gather | solution.py:124
  119.2 12.7 %copy.179 = bf16[512,9216]{0,1:T(8,128)(2,1)} copy(bf16[512,9216]{1,0:T(8,128)(2,1)} %all-gather.2.cloned.1.call-done) | data formatting | bytes 18874368 | tf_op jit(solution)/shard_map/all_gather | solution.py:124
  131.8 7.2 %all-to-all-start = ((bf16[512,16,576]{0,2,1:T(8,128)(2,1)}), bf16[512,16,576]{0,2,1:T(8,128)(2,1)}, u32[]{:S(2)}, u32[]{:S(2)}) async-start(bf16[512,16,576]{0,2,1:T(8,128)(2,1)} %bitcast.111), calls=%async_computation | async-start | bytes 18874368 | tf_op jit(solution)/shard_map/all_to_all | solution.py:125
  139.8 16.0 %reshape.185 = bf16[640,8192]{1,0:T(8,128)(2,1)} reshape(bf16[320,2,8192]{2,1,0:T(2,128)(2,1)} %param.17) | data formatting | bytes 20971520 | tf_op jit(solution)/shard_map/reshape | solution.py:153
  155.9 5.2 multiply_cosine_fusion
  161.1 85.2 %all-to-all-done = bf16[512,16,576]{0,2,1:T(8,128)(2,1)} async-done(((bf16[512,16,576]{0,2,1:T(8,128)(2,1)}), bf16[512,16,576]{0,2,1:T(8,128)(2,1)}, u32[]{:S(2)}, u32[]{:S(2)}) %all-to-all-start) | async-done | bytes 9437216 | tf_op jit(solution)/shard_map/all_to_all | solution.py:125
  246.3 14.1 %copy.180 = bf16[16,512,576]{2,1,0:T(8,128)(2,1)} copy(bf16[16,512,576]{1,2,0:T(8,128)(2,1)} %bitcast.7) | data formatting | bytes 18874368 | tf_op jit(solution)/shard_map/all_to_all | solution.py:125
  260.5 9.3 %copy.181 = bf16[8,16,64,576]{3,2,1,0:T(8,128)(2,1)} copy(bf16[8,16,64,576]{3,2,0,1:T(8,128)(2,1)} %bitcast.110) | data formatting | bytes 18874368 | tf_op jit(solution)/shard_map/transpose | solution.py:126
  269.8 2.2 slice.60
  272.0 2.0 divide_convert_fusion
  274.0 3.0 multiply_convert_fusion
  277.1 9.9 %fusion.16 = f32[640,320]{0,1:T(8,128)S(1)} fusion(bf16[640,8192]{1,0:T(8,128)(2,1)} %reshape.185, bf16[8192,32]{1,0:T(8,128)(2,1)S(1)} %slice.60, bf16[8192,32]{1,0:T(8,128)(2,1)S(1)} %divide_convert_fusion, bf16[8192,256]{1,0:T(8,128)(2,1)S(1)} %multiply_convert_fusion), kind=kOutput, calls=%fused_computation.19 | convolution fusion | flops 3371171840 | bytes 16547840 | tf_op jit(solution)/shard_map/dot_general | solution.py:154
  293.9 4.3 all-to-all-start.1
  298.4 10.9 %all-to-all-done.1 = bf16[16,20,640]{2,1,0:T(8,128)(2,1)S(1)} async-done(((bf16[16,20,640]{2,1,0:T(8,128)(2,1)}), bf16[16,20,640]{2,1,0:T(8,128)(2,1)S(1)}, u32[]{:S(2)}, u32[]{:S(2)}) %all-to-all-start.1) | async-done | bytes 409632 | tf_op jit(solution)/shard_map/all_to_all | solution.py:177
  313.4 1.6 fusion.53
  315.0 4.1 bitcast_reduce_fusion
  320.0 3.4 fusion.22
  323.9 1.7 copy.214
  325.5 4.5 reshape.208
  330.0 12.9 %all_to_all.47 = bf16[16,2,5120]{2,1,0:T(2,128)(2,1)S(1)} all-to-all(bf16[16,2,5120]{2,1,0:T(2,128)(2,1)S(1)} %reshape.208), channel_id=1, replica_groups=mesh['rep'=8,'tp'=16] {'tp'}, dimensions={0} | all-to-all | bytes 655360 | tf_op jit(solution)/shard_map/all_to_all | solution.py:186
  342.9 5.2 reshape.209
  349.7 13.4 %fusion.10 = f32[8192,640]{1,0:T(8,128)} fusion(bf16[640,256]{1,0:T(8,128)(2,1)S(1)} %reshape.196, bf16[8192,576]{1,0:T(8,128)(2,1)} %bitcast.109), kind=kOutput, calls=%fused_computation.11 | convolution fusion | flops 2684354560 | bytes 25493504 | tf_op jit(solution)/shard_map/dot_general | solution.py:189
  363.1 162.8 %reduce-scatter.2.cloned.1.call-done = f32[512,640]{1,0:T(8,128)} async-done(((f32[8192,640]{1,0:T(8,128)}), f32[512,640]{1,0:T(8,128)}) %reduce-scatter.2.cloned.1.call-update) | async-done | bytes 1310736 | tf_op jit(solution)/shard_map/reduce_scatter | solution.py:188
  (78 shorter events, 22.7 us)
Async XLA Ops:
  6.5 112.6 %all-gather.2.cloned.1.call-start = ((), (), s32[]{:S(2)}) async-start(), calls=%async_computation.4 | async-start | bytes 10616832 | tf_op jit(solution)/shard_map/all_gather | solution.py:124
  131.8 7.2 %copy-start.1 = (f32[512]{0:T(512)S(1)}, f32[512]{0:T(512)}, u32[]{:S(2)}) copy-start(f32[512]{0:T(512)} %param.16) | copy-start | bytes 6148
  131.8 7.3 %copy-start = (f32[4096]{0:T(1024)S(1)}, f32[4096]{0:T(1024)}, u32[]{:S(2)}) copy-start(f32[4096]{0:T(1024)} %param.15) | copy-start | bytes 49156
  131.8 7.8 %copy-start.2 = (s32[320]{0:T(512)S(1)}, s32[320]{0:T(512)}, u32[]{:S(2)}) copy-start(s32[320]{0:T(512)} %param.18) | copy-start | bytes 3844
  131.8 114.5 %all-to-all-start = ((bf16[512,16,576]{0,2,1:T(8,128)(2,1)}), bf16[512,16,576]{0,2,1:T(8,128)(2,1)}, u32[]{:S(2)}, u32[]{:S(2)}) async-start(bf16[512,16,576]{0,2,1:T(8,128)(2,1)} %bitcast.111), calls=%async_computation | async-start | bytes 18874368 | tf_op jit(solution)/shard_map/all_to_all | solution.py:125
  288.7 9.6 %copy-start.3 = (s32[20]{0:T(128)S(1)}, s32[20]{0:T(128)}, u32[]{:S(2)}) copy-start(s32[20]{0:T(128)} %param.21) | copy-start | bytes 244
  293.9 15.3 %all-to-all-start.1 = ((bf16[16,20,640]{2,1,0:T(8,128)(2,1)}), bf16[16,20,640]{2,1,0:T(8,128)(2,1)S(1)}, u32[]{:S(2)}, u32[]{:S(2)}) async-start(bf16[16,20,640]{2,1,0:T(8,128)(2,1)} %all_to_all.38), calls=%async_computation.1 | async-start | bytes 983040 | tf_op jit(solution)/shard_map/all_to_all | solution.py:177
  298.2 227.6 %reduce-scatter.2.cloned.1.call-start = ((), (), s32[]{:S(2)}) async-start(), calls=%async_computation.5 | async-start | bytes 22282240 | tf_op jit(solution)/shard_map/reduce_scatter | solution.py:188
Sparse Core Ops, SparseCore 0:
  14.0 105.1 all-gather.1
  363.2 162.6 reduce-scatter.1
where the time goes:
time: 537 us; the launch traced here: 535 us
  waiting for transfers between devices  364 us (68%)
  local copies, waits for them, and re-layouts  83.3 us (16%)
  matrix products  32.8 us (6%)
  other arithmetic  16.8 us (3%)
  between operations  13.8 us (3%)
  blocking collectives  12.9 us (2%)
  starting transfers between devices  11.6 us (2%)
    reduce_scatter x1, waiting for transfers between devices, body(): lax.psum_scatter(lax.dot_general(output_local, head_rows, (((1,), (1,)),...  163 us
    all_gather x1, waiting for transfers between devices, body(): group_rows = lax.all_gather(packed, 'rep', axis=0, tiled=True)  105 us
    all_to_all x1, waiting for transfers between devices, body(): lax.all_to_all(group_rows, 'tp', split_axis=1, concat_axis=0, tiled=True)  85.2 us
    reshape x1, local copies, waits for them, and re-layouts, body(): flat_rows = hidden.reshape(seq_count * 2, model_width)  16 us
    unnamed x16, local copies, waits for them, and re-layouts  14.2 us
    all_to_all x1, local copies, waits for them, and re-layouts, body(): lax.all_to_all(group_rows, 'tp', split_axis=1, concat_axis=0, tiled=True)  14.1 us
    dot_general x1, matrix products, body(): lax.dot_general(output_local, head_rows, (((1,), (1,)), ((), ())), prefer...  13.4 us
    all_to_all x1, blocking collectives, body(): lax.all_to_all(mixed_heads, 'tp', split_axis=2, concat_axis=0, tiled=True)  12.9 us
  transfers between devices with their start and end apart: 4, of which 4 were waited for; matrix products, arithmetic and copies ran while one was open for 4% of the time, Pallas kernels for 0%

commit v1 on v0

--- a/solution.py
+++ b/solution.py
@@ -83,17 +83,6 @@
     piece_width = pieces.shape[-1] // 2
     shaped = pieces.reshape(held_seqs, KVH, duplicate, 2, 2, piece_width)
     return jnp.transpose(shaped, (0, 3, 1, 4, 2, 5)).reshape(held_seqs, 2, KVH, HD)
-
-
-def bundle(query_weight, key_weight, value_weight, output_weight, tp_count):
-    row_count = query_weight.shape[0]
-    parts_list = [
-        query_weight.reshape(row_count, tp_count, -1),
-        pair_split(key_weight, tp_count),
-        pair_split(value_weight, tp_count),
-        output_weight.reshape(row_count, tp_count, -1),
-    ]
-    return jnp.concatenate(parts_list, axis=2).reshape(row_count, -1)
 
 
 def body(
@@ -119,15 +108,28 @@
     heads_here = HQ // tp_count
     split_at = q_width + 2 * kv_width
     factor = smoothing(query_amax, key_amax)
-    packed = bundle(query_weight, key_weight, value_weight, output_weight, tp_count)
-    shard_rows = packed.shape[0]
-    group_rows = lax.all_gather(packed, "rep", axis=0, tiled=True)
-    spread = lax.all_to_all(group_rows, "tp", split_axis=1, concat_axis=0, tiled=True)
-    delivered = jnp.swapaxes(spread.reshape(tp_count, rep_count, shard_rows, -1), 0, 1).reshape(
-        tp_count * rep_count * shard_rows, -1
+    shard_rows = query_weight.shape[0]
+    packed = jnp.concatenate(
+        [
+            query_weight.reshape(shard_rows, tp_count, -1),
+            pair_split(key_weight, tp_count),
+            pair_split(value_weight, tp_count),
+        ],
+        axis=2,
+    )
+    spread = lax.all_to_all(packed, "tp", split_axis=1, concat_axis=0, tiled=True)
+    delivered = lax.all_gather(
+        spread.reshape(tp_count * shard_rows, split_at), "rep", axis=0, tiled=True
     )
     model_width = delivered.shape[0]
-    output_local = delivered[:, split_at:]
+    routes = [
+        (r * tp_count + t, (t % rep_count) * tp_count + (r * tp_count + t) // rep_count)
+        for r in range(rep_count)
+        for t in range(tp_count)
+    ]
+    output_local = lax.all_gather(
+        lax.ppermute(output_weight, ("rep", "tp"), routes), "rep", axis=0, tiled=True
+    )
     group_size = HQ // KVH
     head_factor = lax.dynamic_slice_in_dim(
         jnp.repeat(factor, group_size, axis=0), tp_rank * heads_here, heads_here, 0
@@ -147,7 +149,7 @@
         jnp.bfloat16
     )
     projection = jnp.concatenate(
-        [query_cols, key_cols, delivered[:, q_width + kv_width : split_at]], axis=1
+        [query_cols, key_cols, delivered[:, q_width + kv_width :]], axis=1
     )
     seq_count = hidden.shape[0]
     flat_rows = hidden.reshape(seq_count * 2, model_width)
@@ -183,17 +185,13 @@
     key_all = natural_order(arranged[..., q_width : q_width + kv_width], duplicate)
     value_all = natural_order(arranged[..., q_width + kv_width :], duplicate)
     mixed_heads = attend(query_all, key_all, value_all, cache_keys, cache_values, lengths)
-    gathered_heads = lax.all_to_all(mixed_heads, "tp", split_axis=2, concat_axis=0, tiled=True)
-    head_rows = gathered_heads.reshape(seq_count * 2, q_width)
-    summed = lax.psum_scatter(
-        lax.dot_general(
-            output_local, head_rows, (((1,), (1,)), ((), ())), preferred_element_type=jnp.float32
-        ),
-        "tp",
-        scatter_dimension=0,
-        tiled=True,
-    )
-    return jnp.transpose(summed).astype(jnp.bfloat16).reshape(seq_count, 2, -1)
+    gathered_heads = lax.all_gather(
+        mixed_heads.reshape(held_seqs * 2, HQ * HD), "tp", axis=0, tiled=True
+    )
+    result = lax.dot_general(
+        gathered_heads, output_local, (((1,), (1,)), ((), ())), preferred_element_type=jnp.float32
+    )
+    return result.astype(jnp.bfloat16).reshape(seq_count, 2, -1)
 
 
 def solution(mesh):

time: 537 us -> 256 us (0.48)
  waiting for transfers between devices: 364 us -> 136 us
  local copies, waits for them, and re-layouts: 83.3 us -> 32.9 us
  blocking collectives: 12.9 us -> 22.6 us
  matrix products: 32.8 us -> 26.1 us
    reduce_scatter x1 -> x0, waiting for transfers between devices: 163 us -> none  [body(): lax.psum_scatter(lax.dot_general(output_local, head_rows, (((1,), (1,)),...]
    all_to_all x1 -> x0, waiting for transfers between devices: 85.2 us -> none  [body(): lax.all_to_all(group_rows, 'tp', split_axis=1, concat_axis=0, tiled=True)]
    all_to_all x2 -> x0, local copies, waits for them, and re-layouts: 15.6 us -> none  [the longest x1 14.1 us: body(): lax.all_to_all(group_rows, 'tp', split_axis=1, concat_axis=0, tiled=True)]
    all_gather x1 -> x0, local copies, waits for them, and re-layouts: 12.7 us -> none  [body(): group_rows = lax.all_gather(packed, 'rep', axis=0, tiled=True)]
    unnamed x16 -> x18, local copies, waits for them, and re-layouts: 14.2 us -> 3.01 us
    all_to_all x1, blocking collectives: 12.9 us -> 22.6 us  [body(): lax.all_to_all(packed, 'tp', split_axis=1, concat_axis=0, tiled=True)]
    transpose x1 -> x0, local copies, waits for them, and re-layouts: 9.34 us -> none  [body(): jnp.swapaxes(spread.reshape(tp_count, rep_count, shard_rows, -1), 0, 1)]
    ppermute x0 -> x1, waiting for transfers between devices: none -> 7.72 us  [body(): lax.ppermute(output_weight, ('rep', 'tp'), routes)]
  transfers between devices with their start and end apart: 4 -> 5, of which waited for: 4 -> 4; matrix products, arithmetic and copies ran while one was open for 4% -> 23% of each run, Pallas kernels for 0% -> 0%
where the time goes in v1:
time: 256 us; the launch traced here: 255 us
  waiting for transfers between devices  136 us (53%)
  local copies, waits for them, and re-layouts  32.9 us (13%)
  matrix products  26.1 us (10%)
  blocking collectives  22.6 us (9%)
  between operations  13.6 us (5%)
  other arithmetic  13.2 us (5%)
  starting transfers between devices  11 us (4%)
    all_gather x1, waiting for transfers between devices, body(): lax.all_gather(mixed_heads.reshape(held_seqs * 2, HQ * HD), 'tp', axis=0,...  60.2 us
    all_gather x1, waiting for transfers between devices, body(): lax.all_gather(spread.reshape(tp_count * shard_rows, split_at), 'rep', ax...  51.2 us
    all_to_all x1, blocking collectives, body(): lax.all_to_all(packed, 'tp', split_axis=1, concat_axis=0, tiled=True)  22.6 us
    all_to_all x1, waiting for transfers between devices, body(): lax.all_to_all(outgoing, 'tp', split_axis=0, concat_axis=1, tiled=True)  16.6 us
    reshape x1, local copies, waits for them, and re-layouts, body(): flat_rows = hidden.reshape(seq_count * 2, model_width)  16.1 us
    dot_general x1, matrix products, body(): jnp.dot(flat_rows, projection, preferred_element_type=jnp.float32)  9.94 us
    ppermute x1, waiting for transfers between devices, body(): lax.ppermute(output_weight, ('rep', 'tp'), routes)  7.72 us
    dot_general x1, matrix products, body(): lax.dot_general(gathered_heads, output_local, (((1,), (1,)), ((), ())), p...  6.66 us
  transfers between devices with their start and end apart: 5, of which 4 were waited for; matrix products, arithmetic and copies ran while one was open for 23% of the time, Pallas kernels for 0%

profile of v1, /device:TPU:1, one launch (start us, length us, event | category | flops | bytes accessed | tf_op | source)
XLA Modules:
  0.0 255.2 jit_solution(8600685524332212122)
XLA Ops:
  6.6 1.1 copy.160
  7.7 1.0 copy.101
  8.9 1.0 copy.103
  10.3 22.6 %all_to_all.31 = bf16[64,16,320]{2,0,1:T(8,128)(2,1)} all-to-all(bf16[64,16,320]{2,0,1:T(8,128)(2,1)S(1)} %pad_maximum_fusion), channel_id=1, replica_groups=mesh['rep'=8,'tp'=16] {'tp'}, dimensions={1} | all-to-all | bytes 1310720 | tf_op jit(solution)/shard_map/all_to_all | solution.py:120
  33.0 4.4 %collective-permute-start = (bf16[64,4096]{1,0:T(8,128)(2,1)S(1)}, bf16[64,4096]{1,0:T(8,128)(2,1)S(1)}, u32[]{:S(2)}, u32[]{:S(2)}) collective-permute-start(bf16[64,4096]{1,0:T(8,128)(2,1)S(1)} %copy-done.6), channel_id=1, source_target_pairs={{0,0},{1,16},{2,32},{3,48},{4,64},{5,80},{6,96},{7,112},{8,1},{9,1... | collective-permute-start | bytes 1572872 | tf_op jit(solution)/shard_map/ppermute | solution.py:131
  38.0 16.1 %reshape.163 = bf16[640,8192]{1,0:T(8,128)(2,1)} reshape(bf16[320,2,8192]{2,1,0:T(2,128)(2,1)} %param.17) | data formatting | bytes 20971520 | tf_op jit(solution)/shard_map/reshape | solution.py:155
  54.3 5.4 %multiply_cosine_fusion = (f32[320,2,64]{2,1,0:T(2,128)S(1)}, f32[320,2,64]{2,1,0:T(2,128)S(1)}) fusion(f32[64]{0:T(128)S(1)} %multiply_power_fusion.1, f32[320,2]{1,0:T(8,128)S(1)} %copy.112), kind=kLoop, calls=%fused_computation.36 | loop fusion | flops 40960 | bytes 330496 | tf_op jit(solution)/shard_map/cos | solution.py:27
  59.7 7.7 %collective-permute-done = bf16[64,4096]{1,0:T(8,128)(2,1)S(1)} collective-permute-done((bf16[64,4096]{1,0:T(8,128)(2,1)S(1)}, bf16[64,4096]{1,0:T(8,128)(2,1)S(1)}, u32[]{:S(2)}, u32[]{:S(2)}) %collective-permute-start) | collective-permute-done | bytes 524320 | tf_op jit(solution)/shard_map/ppermute | solution.py:131
  68.2 51.2 %all-gather.4.cloned.1.call-done = bf16[8192,320]{1,0:T(8,128)(2,1)} async-done(((bf16[1024,320]{1,0:T(8,128)(2,1)}), bf16[8192,320]{1,0:T(8,128)(2,1)}) %all-gather.4.cloned.1.call-update) | async-done | bytes 5242896 | tf_op jit(solution)/shard_map/all_gather | solution.py:121
  119.5 2.1 divide_convert_fusion
  121.6 2.5 slice.55
  125.0 9.9 %fusion.14 = f32[640,320]{0,1:T(8,128)S(1)} fusion(bf16[640,8192]{1,0:T(8,128)(2,1)} %reshape.163, bf16[8192,32]{1,0:T(8,128)(2,1)S(1)} %slice.55, bf16[8192,32]{1,0:T(8,128)(2,1)S(1)} %divide_convert_fusion, bf16[8192,256]{1,0:T(8,128)(2,1)S(1)} %multiply_convert_fusion), kind=kOutput, calls=%fused_computation.17 | convolution fusion | flops 3371171840 | bytes 16547840 | tf_op jit(solution)/shard_map/dot_general | solution.py:156
  137.1 1.0 subtract_convert_fusion
  138.1 0.9 pad_maximum_fusion.2
  139.4 1.2 pad_maximum_fusion.1
  140.6 1.2 all_to_all.26
  141.9 6.5 %all-to-all-start.1 = ((bf16[16,20,640]{2,1,0:T(8,128)(2,1)}), bf16[16,20,640]{2,1,0:T(8,128)(2,1)S(1)}, u32[]{:S(2)}, u32[]{:S(2)}) async-start(bf16[16,20,640]{2,1,0:T(8,128)(2,1)} %all_to_all.26), calls=%async_computation.1 | async-start | bytes 983040 | tf_op jit(solution)/shard_map/all_to_all | solution.py:179
  148.4 16.6 %all-to-all-done.1 = bf16[16,20,640]{2,1,0:T(8,128)(2,1)S(1)} async-done(((bf16[16,20,640]{2,1,0:T(8,128)(2,1)}), bf16[16,20,640]{2,1,0:T(8,128)(2,1)S(1)}, u32[]{:S(2)}, u32[]{:S(2)}) %all-to-all-start.1) | async-done | bytes 409632 | tf_op jit(solution)/shard_map/all_to_all | solution.py:179
  169.1 1.6 fusion.51
  170.7 4.1 %bitcast_reduce_fusion = (f32[20,2,4,8]{3,1,2,0:T(2,128)S(1)}, f32[20,4,2,8,256]{4,3,2,1,0:T(8,128)S(1)}) fusion(bf16[20,4,256,128]{3,2,1,0:T(8,128)(2,1)} %param.19, bf16[20,2,4,8,128]{4,3,2,1,0:T(8,128)(2,1)S(1)} %bitcast.106, pred[20,256]{1,0:T(8,128)(4,1)S(1)} %iota_compare_fusion), kind=kOutput, calls=%fused_computation.15 | convolution fusion | flops 84867840 | bytes 6891520 | tf_op jit(solution)/shard_map/btghd,bgld->btghl/dot_general | solution.py:41
  175.8 3.4 %fusion.20 = f32[20,2,4,8,128]{4,3,1,2,0:T(8,128)S(1)} fusion(bf16[20,4,256,128]{3,2,1,0:T(8,128)(2,1)} %param.20, f32[20,4,2,8,256]{4,3,2,1,0:T(8,128)S(1)} %get-tuple-element.16, f32[20,2,4,8]{3,1,2,0:T(2,128)S(1)} %max.7), kind=kOutput, calls=%fused_computation.19 | convolution fusion | flops 84541440 | bytes 7214080 | tf_op jit(solution)/shard_map/btghl,bgld->btghd/dot_general | solution.py:58
  180.7 60.2 %all-gather.6.cloned.1.call-done = bf16[640,4096]{1,0:T(8,128)(2,1)} async-done(((bf16[40,4096]{1,0:T(8,128)(2,1)}), bf16[640,4096]{1,0:T(8,128)(2,1)}) %all-gather.6.cloned.1.call-update) | async-done | bytes 5242896 | tf_op jit(solution)/shard_map/all_gather | solution.py:188
  240.9 6.7 %convolution_convert_fusion = bf16[640,512]{1,0:T(8,128)(2,1)S(1)} fusion(bf16[640,4096]{1,0:T(8,128)(2,1)} %all-gather.6.cloned.1.call-done, bf16[512,4096]{1,0:T(8,128)(2,1)} %all-gather.8.cloned.1.call-done), kind=kOutput, calls=%fused_computation.13 | convolution fusion | flops 2684682240 | bytes 10092544 | tf_op jit(solution)/shard_map/dot_general | solution.py:191
  247.5 1.1 reshape.173
  (77 shorter events, 12.0 us)
Async XLA Ops:
  6.5 26.4 %copy-start.6 = (bf16[64,4096]{1,0:T(8,128)(2,1)S(1)}, bf16[64,4096]{1,0:T(8,128)(2,1)}, u32[]{:S(2)}) copy-start(bf16[64,4096]{1,0:T(8,128)(2,1)} %param.14) | copy-start | bytes 1572868
  6.5 30.9 %copy-start.2 = (f32[4096]{0:T(1024)S(1)}, f32[4096]{0:T(1024)}, u32[]{:S(2)}) copy-start(f32[4096]{0:T(1024)} %param.15) | copy-start | bytes 49156
  6.5 31.0 %copy-start.3 = (f32[512]{0:T(512)S(1)}, f32[512]{0:T(512)}, u32[]{:S(2)}) copy-start(f32[512]{0:T(512)} %param.16) | copy-start | bytes 6148
  6.5 31.2 %copy-start.4 = (s32[320]{0:T(512)S(1)}, s32[320]{0:T(512)}, u32[]{:S(2)}) copy-start(s32[320]{0:T(512)} %param.18) | copy-start | bytes 3844
  6.5 112.9 %all-gather.4.cloned.1.call-start = ((), (), s32[]{:S(2)}) async-start(), calls=%async_computation.2 | async-start | bytes 7077888 | tf_op jit(solution)/shard_map/all_gather | solution.py:121
  32.9 147.8 %all-gather.8.cloned.1.call-start = ((), (), s32[]{:S(2)}) async-start(), calls=%async_computation.4 | async-start | bytes 4718592 | tf_op jit(solution)/shard_map/all_gather | solution.py:130
  33.0 34.4 %collective-permute-start = (bf16[64,4096]{1,0:T(8,128)(2,1)S(1)}, bf16[64,4096]{1,0:T(8,128)(2,1)S(1)}, u32[]{:S(2)}, u32[]{:S(2)}) collective-permute-start(bf16[64,4096]{1,0:T(8,128)(2,1)S(1)} %copy-done.6), channel_id=1, source_target_pairs={{0,0},{1,16},{2,32},{3,48},{4,64},{5,80},{6,96},{7,112},{8,1},{9,1... | collective-permute-start | bytes 1572872 | tf_op jit(solution)/shard_map/ppermute | solution.py:131
  67.4 0.8 copy-start.1
  119.5 4.7 %copy-start = (bf16[8192,320]{1,0:T(8,128)(2,1)S(1)}, bf16[8192,320]{1,0:T(8,128)(2,1)}, u32[]{:S(2)}) copy-start(bf16[8192,320]{1,0:T(8,128)(2,1)} %all-gather.4.cloned.1.call-done) | copy-start | bytes 15728644
  137.1 11.3 %copy-start.5 = (s32[20]{0:T(128)S(1)}, s32[20]{0:T(128)}, u32[]{:S(2)}) copy-start(s32[20]{0:T(128)} %param.21) | copy-start | bytes 244
  141.9 23.2 %all-to-all-start.1 = ((bf16[16,20,640]{2,1,0:T(8,128)(2,1)}), bf16[16,20,640]{2,1,0:T(8,128)(2,1)S(1)}, u32[]{:S(2)}, u32[]{:S(2)}) async-start(bf16[16,20,640]{2,1,0:T(8,128)(2,1)} %all_to_all.26), calls=%async_computation.1 | async-start | bytes 983040 | tf_op jit(solution)/shard_map/all_to_all | solution.py:179
  148.3 92.6 %all-gather.6.cloned.1.call-start = ((), (), s32[]{:S(2)}) async-start(), calls=%async_computation.3 | async-start | bytes 5570560 | tf_op jit(solution)/shard_map/all_gather | solution.py:188
Sparse Core Ops, SparseCore 0:
  33.0 86.3 all-gather.3
  121.1 58.6 all-gather.7
  182.2 58.6 all-gather.5

commit v2 on v1

v2 whole, which is shorter than its diff:
```python
import jax
import jax.numpy as jnp
from jax import lax
from jax.experimental import pallas as pl
from jax.experimental.pallas import tpu as pltpu
from jax.sharding import PartitionSpec as P

D = 8192
HQ = 32
KVH = 4
HD = 128
LMAX = 256
REP = 8
TP = 16
ROWS = D // (REP * TP)
SEQS = 20
TOKENS = 2 * SEQS
ALL_ROWS = TP * TOKENS
MAIN = 32
TAIL = TOKENS - MAIN
Q_ROWS = SEQS * 16
ROPE_THETA = 1000000.0
MESH = pl.DeviceIdType.MESH
BF = jnp.bfloat16
F32 = jnp.float32


def iota(shape, dim):
    return lax.broadcasted_iota(jnp.int32, shape, dim)


def swap_halves(x):
    return pltpu.roll(x, HD // 2, 1)


def top_half(view):
    return view.at[pl.ds(0, view.shape[0] // 2)]


def bottom_half(view):
    return view.at[pl.ds(view.shape[0] // 2, view.shape[0] // 2)]


def left_half(view):
    return view.at[:, pl.ds(0, view.shape[1] // 2)]


def right_half(view):
    return view.at[:, pl.ds(view.shape[1] // 2, view.shape[1] // 2)]


BY_ROWS = (lambda view: view, top_half, bottom_half)
BY_LANES = (lambda view: view, left_half, right_half)


class Gather:
    ARRIVES = (
        ("x", 0), ("m", 0), ("p", 0), ("xm", 0), ("xp", 0),
        ("2", 1), ("2", 2), ("x2", 1), ("x2", 2),
    )
    SENT = (
        ("own", 0, "x"), ("own", 0, "p"), ("own", 0, "m"), ("x", 0, "p"), ("x", 0, "m"),
        ("m", 1, "p"), ("p", 2, "m"), ("2", 1, "x"), ("2", 2, "x"),
    )

    def __init__(self, buffers, parts, blocks, neighbours, send_sems, recv_sems):
        self.buffers = buffers
        self.parts = parts
        self.blocks = blocks
        self.neighbours = neighbours
        self.send_sems = send_sems
        self.recv_sems = recv_sems

    def copies(self, step, arriving):
        if arriving:
            name, part = self.ARRIVES[step]
            device = self.neighbours["x"]
        else:
            name, part, to = self.SENT[step]
            device = self.neighbours[to]
        for b, (buffer, parts) in enumerate(zip(self.buffers, self.parts)):
            view = parts[part](buffer.at[self.blocks[name]])
            yield pltpu.make_async_remote_copy(
                src_ref=view,
                dst_ref=view,
                send_sem=self.send_sems.at[b, step],
                recv_sem=self.recv_sems.at[b, step],
                device_id=device,
                device_id_type=MESH,
            )

    def send(self, *steps):
        for step in steps:
            for copy in self.copies(step, False):
                copy.start()

    def arrive(self, *steps):
        for step in steps:
            for copy in self.copies(step, True):
                copy.wait_recv()

    def finish(self):
        for step in range(9):
            for copy in self.copies(step, False):
                copy.wait_send()


def kernel(
    wq_ref, wk_ref, wv_ref, wo_ref, qa_ref, ka_ref, hid_ref, pos_ref, ck_ref, cv_ref, len_ref,
    out_ref,
    qf, kvf, wq, kvw, wo, hid, stage, ck, cv, outgoing, incoming, att, tail, tail_f32,
    acc, cosine, sine, pick, unpick, q_g, scores, probs, mixed,
    stage_sems, cache_sems, a_send, a_recv, w_send, w_recv, qkv_send, qkv_recv,
    gq_send, gq_recv, go_send, go_recv, ga_send, ga_recv, core_send, core_recv,
):
    r = lax.axis_index("rep")
    t = lax.axis_index("tp")

    x_rep = lax.rem(r + 4, 8)
    base = r // 4 * 4
    other = 4 - base
    z = lax.rem(r, 4)
    zp, zm, z2 = lax.rem(z + 1, 4), lax.rem(z + 3, 4), lax.rem(z + 2, 4)
    rep_blocks = {
        "own": r, "x": x_rep, "p": base + zp, "m": base + zm, "2": base + z2,
        "xp": other + zp, "xm": other + zm, "x2": other + z2,
    }
    rep_neighbours = {"x": (x_rep, t), "p": (base + zp, t), "m": (base + zm, t)}
    y = t // 4
    low = lax.rem(t, 4)
    far = lax.rem(low + 2, 4)
    yp, ym, y2 = lax.rem(y + 1, 4) * 4, lax.rem(y + 3, 4) * 4, lax.rem(y + 2, 4) * 4
    tp_blocks = {
        "own": t, "x": y * 4 + far, "p": yp + low, "m": ym + low, "2": y2 + low,
        "xp": yp + far, "xm": ym + far, "x2": y2 + far,
    }
    tp_neighbours = {k: (r, tp_blocks[k]) for k in ("x", "p", "m")}
    core = t + 1 - 2 * lax.rem(t, 2)
    wo_to = (lax.rem(t, 8), 2 * r + t // 8)
    wo_from = (t // 2, r + 8 * lax.rem(t, 2))
    wo_stays = jnp.logical_and(wo_to[0] == r, wo_to[1] == t)

    barrier = pltpu.get_barrier_semaphore()

    def greet(device):
        pl.semaphore_signal(barrier, inc=1, device_id=device, device_id_type=MESH)

    for k in range(1, TP):
        greet((r, lax.rem(t + k, TP)))
    for device in rep_neighbours.values():
        greet(device)

    @pl.when(jnp.logical_not(wo_stays))
    def _():
        greet(wo_from)

    def hidden_copy(i, slot):
        return pltpu.make_async_copy(
            hid_ref.at[:, :, pl.ds(i * 1024, 1024)], stage.at[slot], stage_sems.at[slot]
        )

    hidden_copy(0, 0).start()
    hidden_copy(1, 1).start()

    factors = []
    for g in range(KVH):
        query_peak = jnp.broadcast_to(
            jnp.max(qa_ref[8 * g : 8 * g + 8, :], axis=0, keepdims=True), (8, HD)
        )
        query_peak = jnp.maximum(query_peak, swap_halves(query_peak))
        key_peak = jnp.broadcast_to(ka_ref[g : g + 1, :], (8, HD))
        key_peak = jnp.maximum(key_peak, swap_halves(key_peak))
        factors.append(jnp.sqrt(key_peak / query_peak)[0:1, :])
    for dst in range(TP):
        factor = jnp.concatenate([factors[dst // 4]] * 2, axis=1)
        qf[dst] = (wq_ref[:, 256 * dst : 256 * dst + 256].astype(F32) * factor).astype(BF)
    for g in range(KVH):
        kvf[g] = (wk_ref[:, HD * g : HD * g + HD].astype(F32) / factors[g]).astype(BF)
        kvf[KVH + g] = wv_ref[:, HD * g : HD * g + HD]

    pl.semaphore_wait(barrier, TP - 1 + 3 + 1 - wo_stays.astype(jnp.int32))

    half = t // 8
    q_rows = pl.ds(pl.multiple_of(t * ROWS, ROWS), ROWS)
    kv_rows = pl.ds(pl.multiple_of(lax.rem(t, 8) * ROWS, ROWS), ROWS)

    def deliver(k, carry):
        dst = lax.rem(t + k, TP)
        pltpu.make_async_remote_copy(
            src_ref=qf.at[dst], dst_ref=wq.at[r, q_rows],
            send_sem=a_send.at[0], recv_sem=a_recv.at[0],
            device_id=(r, dst), device_id_type=MESH,
        ).start()

        @pl.when(lax.rem(dst, 2) == half)
        def _():
            pltpu.make_async_remote_copy(
                src_ref=kvf.at[lax.rem(dst, 4) // 2 * 4 + dst // 4], dst_ref=kvw.at[r, kv_rows],
                send_sem=a_send.at[1], recv_sem=a_recv.at[1],
                device_id=(r, dst), device_id_type=MESH,
            ).start()

        return carry

    lax.fori_loop(1, TP, deliver, 0)
    pltpu.make_async_copy(qf.at[t], wq.at[r, q_rows], a_recv.at[0]).start()
    own_kv = lax.rem(t, 2) == half

    @pl.when(own_kv)
    def _():
        pltpu.make_async_copy(
            kvf.at[lax.rem(t, 4) // 2 * 4 + t // 4], kvw.at[r, kv_rows], a_recv.at[1]
        ).start()

    def wo_copy():
        return pltpu.make_async_remote_copy(
            src_ref=wo_ref, dst_ref=wo.at[wo_to[0]],
            send_sem=w_send, recv_sem=w_recv, device_id=wo_to, device_id_type=MESH,
        )

    @pl.when(jnp.logical_not(wo_stays))
    def _():
        wo_copy().start()

    @pl.when(wo_stays)
    def _():
        pltpu.make_async_copy(wo_ref, wo.at[r], w_recv).start()

    cache_copies = [
        pltpu.make_async_copy(ck_ref, ck, cache_sems.at[0]),
        pltpu.make_async_copy(cv_ref, cv, cache_sems.at[1]),
    ]

    def relayout(i, carry):
        slot = lax.rem(i, 2)
        hidden_copy(i, slot).wait()
        columns = pl.ds(pl.multiple_of(i * 1024, 1024), 1024)
        hid[:, columns] = stage[slot].reshape(ALL_ROWS, 1024)

        @pl.when(i < 6)
        def _():
            hidden_copy(i + 2, slot).start()

        return carry

    lax.fori_loop(0, 8, relayout, 0)

    gather_q = Gather(
        [wq, kvw], [BY_ROWS, BY_ROWS], rep_blocks, rep_neighbours, gq_send, gq_recv
    )
    gather_o = Gather([wo], [BY_ROWS], rep_blocks, rep_neighbours, go_send, go_recv)
    pltpu.make_async_copy(wq.at[r], wq.at[r], a_recv.at[0]).wait()
    pltpu.make_async_copy(kvw.at[r], kvw.at[r], a_recv.at[1]).wait()
    gather_q.send(0, 1, 2)
    for copy in cache_copies:
        copy.start()

    place = jnp.sum(
        jnp.where(
            iota((ALL_ROWS, 320), 0) // 2 == iota((ALL_ROWS, 320), 1),
            pos_ref[...].astype(F32),
            0.0,
        ),
        axis=1,
        keepdims=True,
    ) + lax.rem(iota((ALL_ROWS, 1), 0), 2).astype(F32)
    channel = lax.rem(iota((1, HD), 1), HD // 2).astype(F32)
    angle = place * (ROPE_THETA ** (-2.0 * channel / HD))
    cosine[...] = jnp.cos(angle)
    sine[...] = jnp.sin(angle) * jnp.where(iota((1, HD), 1) < HD // 2, -1.0, 1.0)

    row, col = iota((576, 512), 0), iota((576, 512), 1)
    b, w = row // 16, lax.rem(row, 16)
    source = w // 4 * 128 + lax.rem(w, 2) * TOKENS + 2 * b + lax.rem(w // 2, 2)
    token = lax.rem(row - Q_ROWS + 128, 128)
    col_row, col_dev = lax.rem(col, 128), col // 128
    fresh_row = jnp.logical_and(col_row == 80 + token, token < TOKENS)
    is_key, is_value = row < Q_ROWS + 128, col_dev >= 2
    hit = jnp.where(
        row < Q_ROWS, (col == source).astype(F32),
        jnp.logical_and(fresh_row, is_key != is_value).astype(F32),
    )
    pick[...] = hit.astype(BF)
    row, col = iota((Q_ROWS, 384), 0), iota((Q_ROWS, 384), 1)
    head, token = row // TOKENS, lax.rem(row, TOKENS)
    source = token // 2 * 16 + head // 2 * 4 + lax.rem(token, 2) * 2 + lax.rem(head, 2)
    unpick[...] = (col == source).astype(F32).astype(BF)

    kv_half = lax.rem(t, 2) * 512

    def project(name, first=False):
        block = rep_blocks[name]
        q_at = pl.multiple_of(block * 1024, 1024)
        kv_at = pl.multiple_of(block * 1024 + kv_half, 512)
        for m in range(0, ALL_ROWS, 128):
            q = jnp.dot(hid[m : m + 128, pl.ds(q_at, 1024)], wq[block], preferred_element_type=F32)
            kv = jnp.dot(hid[m : m + 128, pl.ds(kv_at, 512)], kvw[block], preferred_element_type=F32)
            if first:
                acc[m : m + 128, 0:256] = q
                acc[m : m + 128, 256:384] = kv
            else:
                acc[m : m + 128, 0:256] += q
                acc[m : m + 128, 256:384] += kv

    project("own", True)
    gather_q.arrive(1)
    gather_q.send(5)
    gather_q.arrive(2)
    gather_q.send(6)
    gather_q.arrive(0)
    gather_q.send(3, 4)
    project("m")
    project("p")
    project("x")
    gather_q.arrive(5)
    gather_q.send(7)
    gather_q.arrive(6)
    gather_q.send(8)
    pltpu.make_async_copy(wo.at[r], wo.at[r], w_recv).wait()
    gather_o.send(0, 1, 2)
    project("2")
    gather_q.arrive(3)
    project("xm")
    gather_q.arrive(4)
    project("xp")
    gather_q.arrive(7, 8)
    project("x2")

    is_value_device = lax.rem(t // 2, 2) == 1

    def spread(k, carry):
        dst = lax.rem(t + k, TP)
        rows = pl.ds(pl.multiple_of(dst * TOKENS, 8), TOKENS)
        c, s = cosine[rows, :], sine[rows, :]
        q0, q1, kv = acc[rows, 0:128], acc[rows, 128:256], acc[rows, 256:384]
        q0 = q0 * c + swap_halves(q0) * s
        q1 = q1 * c + swap_halves(q1) * s
        kv = jnp.where(is_value_device, kv, kv * c + swap_halves(kv) * s)
        packed = jnp.concatenate([q0, q1, kv, jnp.zeros((8, HD), F32)], axis=0).astype(BF)

        outgoing[dst] = packed

        @pl.when(k < TP)
        def _():
            pltpu.make_async_remote_copy(
                src_ref=outgoing.at[dst], dst_ref=incoming.at[t],
                send_sem=qkv_send, recv_sem=qkv_recv,
                device_id=(r, dst), device_id_type=MESH,
            ).start()

        @pl.when(k == TP)
        def _():
            pltpu.make_async_copy(outgoing.at[dst], incoming.at[t], qkv_recv).start()

        return carry

    lax.fori_loop(1, TP + 1, spread, 0)
    gather_o.arrive(1)
    gather_o.send(5)
    gather_o.arrive(2)
    gather_o.send(6)
    gather_o.arrive(0)
    gather_o.send(3, 4)

    for copy in cache_copies:
        copy.wait()
    pltpu.make_async_copy(incoming, incoming, qkv_recv).wait()

    lengths = jnp.sum(
        jnp.where(
            iota((Q_ROWS, SEQS), 0) // 16 == iota((Q_ROWS, SEQS), 1), len_ref[...].astype(F32), 0.0
        ),
        axis=1,
        keepdims=True,
    )
    live = iota((Q_ROWS, LMAX), 1).astype(F32) < lengths
    row, col = iota((Q_ROWS, 128), 0), iota((Q_ROWS, 128), 1)
    fresh_live = jnp.logical_and(
        row // 16 == col // 2, lax.rem(col, 2) <= lax.rem(lax.rem(row, 16) // 2, 2)
    )
    mixed[Q_ROWS:384, :] = jnp.zeros((384 - Q_ROWS, HD), BF)

    def attend(g, carry):
        gathered = incoming[pl.ds(g * 4, 4)].reshape(512, HD)
        ordered = jnp.dot(pick[...], gathered, preferred_element_type=F32).astype(BF)
        q_g[...] = ordered[0:Q_ROWS]
        key_new, value_new = ordered[Q_ROWS : Q_ROWS + 128], ordered[Q_ROWS + 128 :]
        for b in range(SEQS):
            scores[16 * b : 16 * b + 16, :] = lax.dot_general(
                q_g[16 * b : 16 * b + 16, :], ck[b, g], (((1,), (1,)), ((), ())),
                preferred_element_type=F32,
            )
        scale = HD ** (-0.5)
        cached = jnp.where(live, scores[...] * scale, -jnp.inf)
        fresh = lax.dot_general(
            q_g[...], key_new, (((1,), (1,)), ((), ())), preferred_element_type=F32
        )
        fresh = jnp.where(fresh_live, fresh * scale, -jnp.inf)
        top = jnp.maximum(
            jnp.max(cached, axis=1, keepdims=True), jnp.max(fresh, axis=1, keepdims=True)
        )
        cached = jnp.exp(cached - top)
        fresh = jnp.exp(fresh - top)
        total = jnp.sum(cached, axis=1, keepdims=True) + jnp.sum(fresh, axis=1, keepdims=True)
        probs[...] = cached.astype(BF)
        fresh_part = jnp.dot(fresh.astype(BF), value_new, preferred_element_type=F32)
        parts = [
            jnp.dot(probs[16 * b : 16 * b + 16, :], cv[b, g], preferred_element_type=F32)
            for b in range(SEQS)
        ]
        mixed[0:Q_ROWS, :] = (
            (jnp.concatenate(parts, axis=0) + fresh_part) / total
        ).astype(BF)
        by_head = jnp.dot(unpick[...], mixed[...], preferred_element_type=F32)
        lanes = pl.multiple_of(g * 1024, 1024)
        tail_lanes = pl.multiple_of(lax.rem(g, 2) * 1024, 1024)
        tail_rows = pl.multiple_of(g // 2 * 8, 8)
        heads = [by_head[TOKENS * h : TOKENS * h + TOKENS] for h in range(8)]
        att[t, :, pl.ds(lanes, 1024)] = jnp.concatenate([x[:MAIN] for x in heads], axis=1).astype(BF)
        tail_f32[pl.ds(tail_rows, 8), pl.ds(tail_lanes, 1024)] = jnp.concatenate(
            [x[MAIN:] for x in heads], axis=1
        )
        return carry

    lax.fori_loop(0, KVH, attend, 0)
    tail[t] = tail_f32[...].astype(BF)

    gather_a = Gather(
        [att, tail], [BY_ROWS, BY_LANES], tp_blocks, tp_neighbours, ga_send, ga_recv
    )
    names = ("own", "m", "p", "x", "2", "xm", "xp", "x2")

    def to_core(i, block, start):
        for b, buffer in enumerate((att, tail)):
            copy = pltpu.make_async_remote_copy(
                src_ref=buffer.at[block], dst_ref=buffer.at[block],
                send_sem=core_send.at[b, i], recv_sem=core_recv.at[b, i],
                device_id=(r, core), device_id_type=MESH,
            )
            if start == 0:
                copy.start()
            elif start == 1:
                copy.wait_recv()
            else:
                copy.wait_send()

    def share(name):
        to_core(names.index(name), tp_blocks[name], 0)

    gather_a.send(0, 1, 2)
    share("own")
    gather_o.arrive(5)
    gather_o.send(7)
    gather_o.arrive(6)
    gather_o.send(8)
    gather_a.arrive(1)
    gather_a.send(5)
    gather_a.arrive(2)
    gather_a.send(6)
    gather_a.arrive(0)
    gather_a.send(3, 4)
    share("m")
    share("p")
    share("x")
    gather_a.arrive(5)
    gather_a.send(7)
    gather_a.arrive(6)
    gather_a.send(8)
    share("2")
    gather_a.arrive(3)
    share("xm")
    gather_a.arrive(4)
    share("xp")
    gather_a.arrive(7, 8)
    share("x2")
    gather_o.arrive(3, 4, 7, 8)
    flip = 1 - 2 * lax.rem(t, 2)
    for i, name in enumerate(names):
        to_core(i, tp_blocks[name] + flip, 1)

    def output(i, carry):
        main = att[pl.ds(i * 4, 4)].reshape(4 * MAIN, HQ * HD)
        last = tail[pl.ds(i * 4, 4)].reshape(64, HQ * HD // 2)
        full = wo[...].reshape(512, HQ * HD)
        dims = (((1,), (1,)), ((), ()))
        main = lax.dot_general(main, full, dims, preferred_element_type=F32)
        first = lax.dot_general(last, full[:, : HQ * HD // 2], dims, preferred_element_type=F32)
        second = lax.dot_general(last, full[:, HQ * HD // 2 :], dims, preferred_element_type=F32)
        rows = []
        for s in range(4):
            rows.append(main[MAIN * s : MAIN * s + MAIN])
            rows.append(first[16 * s : 16 * s + 8] + second[16 * s + 8 : 16 * s + 16])
        at = pl.ds(pl.multiple_of(i * 160, 160), 160)
        out_ref[at, :] = jnp.concatenate(rows, axis=0).astype(BF)
        return carry

    lax.fori_loop(0, 4, output, 0)

    def sent_q(k, carry):
        dst = lax.rem(t + k, TP)
        pltpu.make_async_copy(qf.at[dst], qf.at[dst], a_send.at[0]).wait()
        pltpu.make_async_copy(outgoing.at[dst], outgoing.at[dst], qkv_send).wait()

        @pl.when(lax.rem(dst, 2) == half)
        def _():
            pltpu.make_async_copy(kvf.at[0], kvf.at[0], a_send.at[1]).wait()

        return carry

    lax.fori_loop(1, TP, sent_q, 0)

    @pl.when(jnp.logical_not(wo_stays))
    def _():
        wo_copy().wait_send()

    gather_q.finish()
    gather_o.finish()
    gather_a.finish()
    for i, name in enumerate(names):
        to_core(i, tp_blocks[name], 2)


def body(
    query_weight, key_weight, value_weight, output_weight, query_amax, key_amax,
    hidden, positions, cache_keys, cache_values, lengths,
):
    vmem = pl.BlockSpec(memory_space=pltpu.VMEM)
    hbm = pl.BlockSpec(memory_space=pl.ANY)
    dma = pltpu.SemaphoreType.DMA
    result = pl.pallas_call(
        kernel,
        out_shape=jax.ShapeDtypeStruct((ALL_ROWS, 512), BF),
        in_specs=[vmem, vmem, vmem, hbm, vmem, vmem, hbm, vmem, hbm, hbm, vmem],
        out_specs=vmem,
        scratch_shapes=[
            pltpu.VMEM((TP, ROWS, 256), BF),
            pltpu.VMEM((2 * KVH, ROWS, HD), BF),
            pltpu.VMEM((REP, TP * ROWS, 256), BF),
            pltpu.VMEM((REP, 8 * ROWS, HD), BF),
            pltpu.VMEM((REP, ROWS, HQ * HD), BF),
            pltpu.VMEM((ALL_ROWS, D), BF),
            pltpu.VMEM((2, 320, 2, 1024), BF),
            pltpu.VMEM((SEQS, KVH, LMAX, HD), BF),
            pltpu.VMEM((SEQS, KVH, LMAX, HD), BF),
            pltpu.VMEM((TP, 128, HD), BF),
            pltpu.VMEM((TP, 128, HD), BF),
            pltpu.VMEM((TP, MAIN, HQ * HD), BF),
            pltpu.VMEM((TP, 2 * TAIL, HQ * HD // 2), BF),
            pltpu.VMEM((2 * TAIL, HQ * HD // 2), F32),
            pltpu.VMEM((ALL_ROWS, 384), F32),
            pltpu.VMEM((ALL_ROWS, HD), F32),
            pltpu.VMEM((ALL_ROWS, HD), F32),
            pltpu.VMEM((576, 512), BF),
            pltpu.VMEM((Q_ROWS, 384), BF),
            pltpu.VMEM((Q_ROWS, HD), BF),
            pltpu.VMEM((Q_ROWS, LMAX), F32),
            pltpu.VMEM((Q_ROWS, LMAX), BF),
            pltpu.VMEM((384, HD), BF),
            dma((2,)), dma((2,)), dma((2,)), dma((2,)), dma, dma, dma, dma,
            dma((2, 9)), dma((2, 9)), dma((1, 9)), dma((1, 9)), dma((2, 9)), dma((2, 9)),
            dma((2, 8)), dma((2, 8)),
        ],
        compiler_params=pltpu.CompilerParams(
            collective_id=0, has_side_effects=True, vmem_limit_bytes=62 * 2**20
        ),
    )(
        query_weight, key_weight, value_weight, output_weight,
        query_amax.reshape(HQ, HD), key_amax.reshape(KVH, HD),
        hidden, positions.reshape(1, -1), cache_keys, cache_values, lengths.reshape(1, -1),
    )
    return result.reshape(hidden.shape[0], 2, 512)


def solution(mesh):
    in_specs = (
        P(("rep", "tp"), None),
        P(("rep", "tp"), None),
        P(("rep", "tp"), None),
        P(("rep", "tp"), None),
        P(),
        P(),
        P("rep", None, None),
        P("rep"),
        P(("rep", "tp"), None, None, None),
        P(("rep", "tp"), None, None, None),
        P(("rep", "tp")),
    )
    out_specs = P("rep", None, "tp")

    def run(*args):
        with jax.sharding.use_abstract_mesh(mesh.abstract_mesh):
            return jax.shard_map(
                body, mesh=mesh, in_specs=in_specs, out_specs=out_specs, check_vma=False
            )(*args)

    return run
```

time: 256 us -> 151 us (0.59)
  Pallas kernels: 0 us -> 147 us
  waiting for transfers between devices: 136 us -> 0 us
  local copies, waits for them, and re-layouts: 32.9 us -> 3.87 us
  matrix products: 26.1 us -> 0 us
  blocking collectives: 22.6 us -> 0 us
  between operations: 13.6 us -> 0.01 us
  other arithmetic: 13.2 us -> 0 us
  starting transfers between devices: 11 us -> 0 us
    pallas_call x0 -> x1, Pallas kernels: none -> 147 us  [body(): pl.pallas_call(kernel, out_shape=jax.ShapeDtypeStruct((ALL_ROWS, 512), BF...]
    all_gather x3 -> x0, waiting for transfers between devices: 111 us -> none  [the longest x1 60.2 us: body(): lax.all_gather(mixed_heads.reshape(held_seqs * 2, HQ * HD), 'tp', axis=0,...]
    dot_general x6 -> x0, matrix products: 26.1 us -> none  [the longest x1 9.94 us: body(): jnp.dot(flat_rows, projection, preferred_element_type=jnp.float32)]
    all_to_all x1 -> x0, blocking collectives: 22.6 us -> none  [body(): lax.all_to_all(packed, 'tp', split_axis=1, concat_axis=0, tiled=True)]
    reshape x16 -> x2, local copies, waits for them, and re-layouts: 22.1 us -> 3.87 us  [the longest x1 2.63 us: body(): return result.reshape(hidden.shape[0], 2, 512)]
    all_to_all x1 -> x0, waiting for transfers between devices: 16.6 us -> none  [body(): lax.all_to_all(outgoing, 'tp', split_axis=0, concat_axis=1, tiled=True)]
    ppermute x1 -> x0, waiting for transfers between devices: 7.72 us -> none  [body(): lax.ppermute(output_weight, ('rep', 'tp'), routes)]
    all_to_all x1 -> x0, starting transfers between devices: 6.45 us -> none  [body(): lax.all_to_all(outgoing, 'tp', split_axis=0, concat_axis=1, tiled=True)]
  transfers between devices with their start and end apart: 5 -> 0, of which waited for: 4 -> 0; matrix products, arithmetic and copies ran while one was open for 23% -> 0% of each run, Pallas kernels for 0% -> 0%
where the time goes in v2:
time: 151 us
  Pallas kernels  147 us (97%)
  local copies, waits for them, and re-layouts  3.87 us (3%)
    pallas_call x1, Pallas kernels, body(): pl.pallas_call(kernel, out_shape=jax.ShapeDtypeStruct((ALL_ROWS, 512), BF...  147 us

profile of v2, /device:TPU:1, one launch (start us, length us, event | category | flops | bytes accessed | tf_op | source)
XLA Modules:
  0.0 151.2 jit_solution(3315239267661205113)
XLA Ops:
  0.0 1.2 reshape.17.pos_ref
  1.2 147.3 %shard_map.109 = bf16[640,512]{1,0:T(8,128)(2,1)} custom-call(bf16[64,4096]{1,0:T(8,128)(2,1)} %wq_ref.1, bf16[64,512]{1,0:T(8,128)(2,1)} %wk_ref.1, bf16[64,512]{1,0:T(8,128)(2,1)} %wv_ref.1, bf16[64,4096]{1,0:T(8,128)(2,1)} %wo_ref.1, f32[32,128]{1,0:T(8,128)} %bitcast.3, f32[4,128]{1,0:T(4,128)} %bitcast.4, bf16[320,2,8192]{2,1,0:T(2,128)(2,1)} %hid_ref.1, ...), custom_call_target="tpu_custom_call" | custom-call | tf_op jit(solution)/shard_map/pallas_call | solution.py:530
  148.6 2.6 %reshape.19 = bf16[320,2,512]{2,1,0:T(2,128)(2,1)} reshape(bf16[640,512]{1,0:T(8,128)(2,1)} %shard_map.109) | data formatting | bytes 1310720 | tf_op jit(solution)/shard_map/reshape | solution.py:571

commit v3 on v2

--- a/solution.py
+++ b/solution.py
@@ -108,8 +108,8 @@
 def kernel(
     wq_ref, wk_ref, wv_ref, wo_ref, qa_ref, ka_ref, hid_ref, pos_ref, ck_ref, cv_ref, len_ref,
     out_ref,
-    qf, kvf, wq, kvw, wo, hid, stage, ck, cv, outgoing, incoming, att, tail, tail_f32,
-    acc, cosine, sine, pick, unpick, q_g, scores, probs, mixed,
+    qf, kvf, wq, kvw, wo_stage, wo, hid, stage, ck, cv, outgoing, incoming, att, tail, tail_f32,
+    acc, cosine, sine, pick, unpick, q_g, scores, probs, mixed, main_out, tail_out,
     stage_sems, cache_sems, a_send, a_recv, w_send, w_recv, qkv_send, qkv_recv,
     gq_send, gq_recv, go_send, go_recv, ga_send, ga_recv, core_send, core_recv,
 ):
@@ -136,10 +136,6 @@
     }
     tp_neighbours = {k: (r, tp_blocks[k]) for k in ("x", "p", "m")}
     core = t + 1 - 2 * lax.rem(t, 2)
-    wo_to = (lax.rem(t, 8), 2 * r + t // 8)
-    wo_from = (t // 2, r + 8 * lax.rem(t, 2))
-    wo_stays = jnp.logical_and(wo_to[0] == r, wo_to[1] == t)
-
     barrier = pltpu.get_barrier_semaphore()
 
     def greet(device):
@@ -147,12 +143,8 @@
 
     for k in range(1, TP):
         greet((r, lax.rem(t + k, TP)))
-    for device in rep_neighbours.values():
-        greet(device)
-
-    @pl.when(jnp.logical_not(wo_stays))
-    def _():
-        greet(wo_from)
+    for k in range(1, REP):
+        greet((lax.rem(r + k, REP), t))
 
     def hidden_copy(i, slot):
         return pltpu.make_async_copy(
@@ -178,7 +170,22 @@
         kvf[g] = (wk_ref[:, HD * g : HD * g + HD].astype(F32) / factors[g]).astype(BF)
         kvf[KVH + g] = wv_ref[:, HD * g : HD * g + HD]
 
-    pl.semaphore_wait(barrier, TP - 1 + 3 + 1 - wo_stays.astype(jnp.int32))
+    pl.semaphore_wait(barrier, TP - 1 + REP - 1)
+
+    def wo_columns(i):
+        return wo_ref.at[:, pl.ds(pl.multiple_of(i * 512, 512), 512)]
+
+    def wo_scatter(k, carry):
+        to = lax.rem(r + k, REP)
+        pltpu.make_async_remote_copy(
+            src_ref=wo_columns(to), dst_ref=wo_stage.at[r],
+            send_sem=w_send.at[0], recv_sem=w_recv.at[0],
+            device_id=(to, t), device_id_type=MESH,
+        ).start()
+        return carry
+
+    lax.fori_loop(1, REP, wo_scatter, 0)
+    pltpu.make_async_copy(wo_columns(r), wo_stage.at[r], w_recv.at[0]).start()
 
     half = t // 8
     q_rows = pl.ds(pl.multiple_of(t * ROWS, ROWS), ROWS)
@@ -212,19 +219,24 @@
             kvf.at[lax.rem(t, 4) // 2 * 4 + t // 4], kvw.at[r, kv_rows], a_recv.at[1]
         ).start()
 
-    def wo_copy():
-        return pltpu.make_async_remote_copy(
-            src_ref=wo_ref, dst_ref=wo.at[wo_to[0]],
-            send_sem=w_send, recv_sem=w_recv, device_id=wo_to, device_id_type=MESH,
-        )
-
-    @pl.when(jnp.logical_not(wo_stays))
-    def _():
-        wo_copy().start()
-
-    @pl.when(wo_stays)
-    def _():
-        pltpu.make_async_copy(wo_ref, wo.at[r], w_recv).start()
+    wo_rows = pl.ds(pl.multiple_of(lax.rem(t, 8) * ROWS, ROWS), ROWS)
+
+    def wo_deliver(i, carry):
+        dst = 2 * i + half
+
+        @pl.when(dst != t)
+        def _():
+            pltpu.make_async_remote_copy(
+                src_ref=wo_stage.at[i], dst_ref=wo.at[r, wo_rows],
+                send_sem=w_send.at[1], recv_sem=w_recv.at[1],
+                device_id=(r, dst), device_id_type=MESH,
+            ).start()
+
+        @pl.when(dst == t)
+        def _():
+            pltpu.make_async_copy(wo_stage.at[i], wo.at[r, wo_rows], w_recv.at[1]).start()
+
+        return carry
 
     cache_copies = [
         pltpu.make_async_copy(ck_ref, ck, cache_sems.at[0]),
@@ -243,8 +255,6 @@
 
         return carry
 
-    lax.fori_loop(0, 8, relayout, 0)
-
     gather_q = Gather(
         [wq, kvw], [BY_ROWS, BY_ROWS], rep_blocks, rep_neighbours, gq_send, gq_recv
     )
@@ -252,8 +262,11 @@
     pltpu.make_async_copy(wq.at[r], wq.at[r], a_recv.at[0]).wait()
     pltpu.make_async_copy(kvw.at[r], kvw.at[r], a_recv.at[1]).wait()
     gather_q.send(0, 1, 2)
+    pltpu.make_async_copy(wo_stage, wo_stage, w_recv.at[0]).wait()
+    lax.fori_loop(0, REP, wo_deliver, 0)
     for copy in cache_copies:
         copy.start()
+    lax.fori_loop(0, 8, relayout, 0)
 
     place = jnp.sum(
         jnp.where(
@@ -268,6 +281,9 @@
     angle = place * (ROPE_THETA ** (-2.0 * channel / HD))
     cosine[...] = jnp.cos(angle)
     sine[...] = jnp.sin(angle) * jnp.where(iota((1, HD), 1) < HD // 2, -1.0, 1.0)
+
+    main_out[...] = jnp.zeros_like(main_out)
+    tail_out[...] = jnp.zeros_like(tail_out)
 
     row, col = iota((576, 512), 0), iota((576, 512), 1)
     b, w = row // 16, lax.rem(row, 16)
@@ -316,14 +332,15 @@
     gather_q.send(7)
     gather_q.arrive(6)
     gather_q.send(8)
-    pltpu.make_async_copy(wo.at[r], wo.at[r], w_recv).wait()
-    gather_o.send(0, 1, 2)
     project("2")
+    pltpu.make_async_copy(wo.at[r], wo.at[r], w_recv.at[1]).wait()
     gather_q.arrive(3)
+    gather_q.arrive(4)
+    gather_o.send(1, 2)
     project("xm")
-    gather_q.arrive(4)
     project("xp")
     gather_q.arrive(7, 8)
+    gather_o.send(0)
     project("x2")
 
     is_value_device = lax.rem(t // 2, 2) == 1
@@ -337,7 +354,6 @@
         q1 = q1 * c + swap_halves(q1) * s
         kv = jnp.where(is_value_device, kv, kv * c + swap_halves(kv) * s)
         packed = jnp.concatenate([q0, q1, kv, jnp.zeros((8, HD), F32)], axis=0).astype(BF)
-
         outgoing[dst] = packed
 
         @pl.when(k < TP)
@@ -355,12 +371,6 @@
         return carry
 
     lax.fori_loop(1, TP + 1, spread, 0)
-    gather_o.arrive(1)
-    gather_o.send(5)
-    gather_o.arrive(2)
-    gather_o.send(6)
-    gather_o.arrive(0)
-    gather_o.send(3, 4)
 
     for copy in cache_copies:
         copy.wait()
@@ -422,7 +432,14 @@
         )
         return carry
 
-    lax.fori_loop(0, KVH, attend, 0)
+    lax.fori_loop(0, 2, attend, 0)
+    gather_o.arrive(1)
+    gather_o.send(5)
+    gather_o.arrive(2)
+    gather_o.send(6)
+    gather_o.arrive(0)
+    gather_o.send(3, 4)
+    lax.fori_loop(2, KVH, attend, 0)
     tail[t] = tail_f32[...].astype(BF)
 
     gather_a = Gather(
@@ -449,10 +466,6 @@
 
     gather_a.send(0, 1, 2)
     share("own")
-    gather_o.arrive(5)
-    gather_o.send(7)
-    gather_o.arrive(6)
-    gather_o.send(8)
     gather_a.arrive(1)
     gather_a.send(5)
     gather_a.arrive(2)
@@ -462,39 +475,66 @@
     share("m")
     share("p")
     share("x")
+    gather_o.arrive(5)
+    gather_o.send(7)
+    gather_o.arrive(6)
+    gather_o.send(8)
     gather_a.arrive(5)
     gather_a.send(7)
     gather_a.arrive(6)
     gather_a.send(8)
     share("2")
+
+    chips = {name: tp_blocks[name] // 2 * 2 for name in names}
+    flip = 1 - 2 * lax.rem(t, 2)
+
+    def from_core(*group):
+        for name in group:
+            to_core(names.index(name), tp_blocks[name] + flip, 1)
+
+    def output(i, group, chunks):
+        for chunk in chunks:
+            block = rep_blocks[chunk]
+            lanes = pl.ds(pl.multiple_of(block * 512, 512), 512)
+            tail_lanes = pl.ds(pl.multiple_of(lax.rem(block, 4) * 512, 512), 512)
+            rows = [att[pl.ds(chips[name], 2), :, lanes].reshape(2 * MAIN, 512) for name in group]
+            rows += [
+                tail[pl.ds(chips[name], 2), :, tail_lanes].reshape(4 * TAIL, 512) for name in group
+            ]
+            product = lax.dot_general(
+                jnp.concatenate(rows, axis=0), wo[block], (((1,), (1,)), ((), ())),
+                preferred_element_type=F32,
+            )
+            main_out[i] += product[:256]
+            tail_out[i, block // 4] += product[256:]
+
+    def store(i, group):
+        for n, name in enumerate(group):
+            rows = []
+            for s in (2 * n, 2 * n + 1):
+                rows.append(main_out[i, MAIN * s : MAIN * s + MAIN, :])
+                rows.append(
+                    tail_out[i, 0, 16 * s : 16 * s + 8, :]
+                    + tail_out[i, 1, 16 * s + 8 : 16 * s + 16, :]
+                )
+            at = pl.ds(pl.multiple_of(chips[name] * TOKENS, 2 * TOKENS), 2 * TOKENS)
+            out_ref[at, :] = jnp.concatenate(rows, axis=0).astype(BF)
+
+    near, distant = ("own", "m", "p", "x"), ("2", "xm", "xp", "x2")
+    from_core(*near)
+    output(0, near, ("own", "m", "p", "x", "2"))
     gather_a.arrive(3)
     share("xm")
     gather_a.arrive(4)
     share("xp")
+    gather_o.arrive(3, 4, 7, 8)
+    output(0, near, ("xm", "xp", "x2"))
     gather_a.arrive(7, 8)
     share("x2")
-    gather_o.arrive(3, 4, 7, 8)
-    flip = 1 - 2 * lax.rem(t, 2)
-    for i, name in enumerate(names):
-        to_core(i, tp_blocks[name] + flip, 1)
-
-    def output(i, carry):
-        main = att[pl.ds(i * 4, 4)].reshape(4 * MAIN, HQ * HD)
-        last = tail[pl.ds(i * 4, 4)].reshape(64, HQ * HD // 2)
-        full = wo[...].reshape(512, HQ * HD)
-        dims = (((1,), (1,)), ((), ()))
-        main = lax.dot_general(main, full, dims, preferred_element_type=F32)
-        first = lax.dot_general(last, full[:, : HQ * HD // 2], dims, preferred_element_type=F32)
-        second = lax.dot_general(last, full[:, HQ * HD // 2 :], dims, preferred_element_type=F32)
-        rows = []
-        for s in range(4):
-            rows.append(main[MAIN * s : MAIN * s + MAIN])
-            rows.append(first[16 * s : 16 * s + 8] + second[16 * s + 8 : 16 * s + 16])
-        at = pl.ds(pl.multiple_of(i * 160, 160), 160)
-        out_ref[at, :] = jnp.concatenate(rows, axis=0).astype(BF)
-        return carry
-
-    lax.fori_loop(0, 4, output, 0)
+    store(0, near)
+    from_core(*distant)
+    output(1, distant, ("own", "m", "p", "x") + distant)
+    store(1, distant)
 
     def sent_q(k, carry):
         dst = lax.rem(t + k, TP)
@@ -509,10 +549,20 @@
 
     lax.fori_loop(1, TP, sent_q, 0)
 
-    @pl.when(jnp.logical_not(wo_stays))
-    def _():
-        wo_copy().wait_send()
-
+    def sent_o(i, carry):
+        pltpu.make_async_copy(wo_stage.at[i], wo_stage.at[i], w_send.at[0]).wait()
+        return carry
+
+    lax.fori_loop(1, REP, sent_o, 0)
+
+    def delivered_o(i, carry):
+        @pl.when(2 * i + half != t)
+        def _():
+            pltpu.make_async_copy(wo_stage.at[i], wo_stage.at[i], w_send.at[1]).wait()
+
+        return carry
+
+    lax.fori_loop(0, REP, delivered_o, 0)
     gather_q.finish()
     gather_o.finish()
     gather_a.finish()
@@ -537,7 +587,8 @@
             pltpu.VMEM((2 * KVH, ROWS, HD), BF),
             pltpu.VMEM((REP, TP * ROWS, 256), BF),
             pltpu.VMEM((REP, 8 * ROWS, HD), BF),
-            pltpu.VMEM((REP, ROWS, HQ * HD), BF),
+            pltpu.VMEM((REP, ROWS, 512), BF),
+            pltpu.VMEM((REP, 512, 512), BF),
             pltpu.VMEM((ALL_ROWS, D), BF),
             pltpu.VMEM((2, 320, 2, 1024), BF),
             pltpu.VMEM((SEQS, KVH, LMAX, HD), BF),
@@ -556,7 +607,9 @@
             pltpu.VMEM((Q_ROWS, LMAX), F32),
             pltpu.VMEM((Q_ROWS, LMAX), BF),
             pltpu.VMEM((384, HD), BF),
-            dma((2,)), dma((2,)), dma((2,)), dma((2,)), dma, dma, dma, dma,
+            pltpu.VMEM((2, 256, 512), F32),
+            pltpu.VMEM((2, 2, 128, 512), F32),
+            dma((2,)), dma((2,)), dma((2,)), dma((2,)), dma((2,)), dma((2,)), dma, dma,
             dma((2, 9)), dma((2, 9)), dma((1, 9)), dma((1, 9)), dma((2, 9)), dma((2, 9)),
             dma((2, 8)), dma((2, 8)),
         ],

time: 151 us -> 131 us (0.87)
  Pallas kernels: 147 us -> 127 us
    pallas_call x1, Pallas kernels: 147 us -> 127 us  [body(): pl.pallas_call(kernel, out_shape=jax.ShapeDtypeStruct((ALL_ROWS, 512), BF...]
where the time goes in v3:
time: 131 us
  Pallas kernels  127 us (97%)
  local copies, waits for them, and re-layouts  3.87 us (3%)
    pallas_call x1, Pallas kernels, body(): pl.pallas_call(kernel, out_shape=jax.ShapeDtypeStruct((ALL_ROWS, 512), BF...  127 us
    reshape x1, local copies, waits for them, and re-layouts, body(): return result.reshape(hidden.shape[0], 2, 512)  2.63 us

profile of v3, /device:TPU:1, one launch (start us, length us, event | category | flops | bytes accessed | tf_op | source)
XLA Modules:
  0.0 130.6 jit_solution(12781162606370944626)
XLA Ops:
  0.0 1.2 reshape.17.pos_ref
  1.2 126.7 %shard_map.109 = bf16[640,512]{1,0:T(8,128)(2,1)} custom-call(bf16[64,4096]{1,0:T(8,128)(2,1)} %wq_ref.1, bf16[64,512]{1,0:T(8,128)(2,1)} %wk_ref.1, bf16[64,512]{1,0:T(8,128)(2,1)} %wv_ref.1, bf16[64,4096]{1,0:T(8,128)(2,1)} %wo_ref.1, f32[32,128]{1,0:T(8,128)} %bitcast.3, f32[4,128]{1,0:T(4,128)} %bitcast.4, bf16[320,2,8192]{2,1,0:T(2,128)(2,1)} %hid_ref.1, ...), custom_call_target="tpu_custom_call" | custom-call | tf_op jit(solution)/shard_map/pallas_call | solution.py:580
  127.9 2.6 %reshape.19 = bf16[320,2,512]{2,1,0:T(2,128)(2,1)} reshape(bf16[640,512]{1,0:T(8,128)(2,1)} %shard_map.109) | data formatting | bytes 1310720 | tf_op jit(solution)/shard_map/reshape | solution.py:624

commit v4 on v3

--- a/solution.py
+++ b/solution.py
@@ -60,26 +60,32 @@
     )
     SENT = (
         ("own", 0, "x"), ("own", 0, "p"), ("own", 0, "m"), ("x", 0, "p"), ("x", 0, "m"),
-        ("m", 1, "p"), ("p", 2, "m"), ("2", 1, "x"), ("2", 2, "x"),
-    )
-
-    def __init__(self, buffers, parts, blocks, neighbours, send_sems, recv_sems):
+        ("m", 1, "p"), ("p", 2, "m"),
+    )
+    LAST = {
+        "pair": (("2", 1, "x"), ("2", 2, "x")),
+        "ring": (("xm", 1, "p"), ("xp", 2, "m")),
+    }
+
+    def __init__(self, buffers, parts, blocks, neighbours, last, send_sems, recv_sems):
+        self.sent = self.SENT + self.LAST[last]
         self.buffers = buffers
         self.parts = parts
         self.blocks = blocks
         self.neighbours = neighbours
         self.send_sems = send_sems
         self.recv_sems = recv_sems
+        self.left = set()
 
     def copies(self, step, arriving):
         if arriving:
             name, part = self.ARRIVES[step]
             device = self.neighbours["x"]
         else:
-            name, part, to = self.SENT[step]
+            name, part, to = self.sent[step]
             device = self.neighbours[to]
         for b, (buffer, parts) in enumerate(zip(self.buffers, self.parts)):
-            view = parts[part](buffer.at[self.blocks[name]])
+            view = parts[part](buffer(self.blocks[name]))
             yield pltpu.make_async_remote_copy(
                 src_ref=view,
                 dst_ref=view,
@@ -99,16 +105,20 @@
             for copy in self.copies(step, True):
                 copy.wait_recv()
 
-    def finish(self):
-        for step in range(9):
+    def leave(self, *steps):
+        for step in steps:
+            self.left.add(step)
             for copy in self.copies(step, False):
                 copy.wait_send()
+
+    def finish(self):
+        self.leave(*(step for step in range(9) if step not in self.left))
 
 
 def kernel(
     wq_ref, wk_ref, wv_ref, wo_ref, qa_ref, ka_ref, hid_ref, pos_ref, ck_ref, cv_ref, len_ref,
     out_ref,
-    qf, kvf, wq, kvw, wo_stage, wo, hid, stage, ck, cv, outgoing, incoming, att, tail, tail_f32,
+    qf, kvf, wq, kvw, wo_stage, wo, hid, stage, ck, cv, outgoing, incoming, att,
     acc, cosine, sine, pick, unpick, q_g, scores, probs, mixed, main_out, tail_out,
     stage_sems, cache_sems, a_send, a_recv, w_send, w_recv, qkv_send, qkv_recv,
     gq_send, gq_recv, go_send, go_recv, ga_send, ga_recv, core_send, core_recv,
@@ -184,8 +194,6 @@
         ).start()
         return carry
 
-    lax.fori_loop(1, REP, wo_scatter, 0)
-    pltpu.make_async_copy(wo_columns(r), wo_stage.at[r], w_recv.at[0]).start()
 
     half = t // 8
     q_rows = pl.ds(pl.multiple_of(t * ROWS, ROWS), ROWS)
@@ -219,6 +227,9 @@
             kvf.at[lax.rem(t, 4) // 2 * 4 + t // 4], kvw.at[r, kv_rows], a_recv.at[1]
         ).start()
 
+    lax.fori_loop(1, REP, wo_scatter, 0)
+    pltpu.make_async_copy(wo_columns(r), wo_stage.at[r], w_recv.at[0]).start()
+
     wo_rows = pl.ds(pl.multiple_of(lax.rem(t, 8) * ROWS, ROWS), ROWS)
 
     def wo_deliver(i, carry):
@@ -256,9 +267,12 @@
         return carry
 
     gather_q = Gather(
-        [wq, kvw], [BY_ROWS, BY_ROWS], rep_blocks, rep_neighbours, gq_send, gq_recv
-    )
-    gather_o = Gather([wo], [BY_ROWS], rep_blocks, rep_neighbours, go_send, go_recv)
+        [lambda block: wq.at[block], lambda block: kvw.at[block]], [BY_ROWS, BY_ROWS], rep_blocks, rep_neighbours,
+        "pair", gq_send, gq_recv,
+    )
+    gather_o = Gather(
+        [lambda block: wo.at[block]], [BY_ROWS], rep_blocks, rep_neighbours, "ring", go_send, go_recv,
+    )
     pltpu.make_async_copy(wq.at[r], wq.at[r], a_recv.at[0]).wait()
     pltpu.make_async_copy(kvw.at[r], kvw.at[r], a_recv.at[1]).wait()
     gather_q.send(0, 1, 2)
@@ -271,7 +285,7 @@
     place = jnp.sum(
         jnp.where(
             iota((ALL_ROWS, 320), 0) // 2 == iota((ALL_ROWS, 320), 1),
-            pos_ref[...].astype(F32),
+            pos_ref[...].reshape(1, TP * SEQS).astype(F32),
             0.0,
         ),
         axis=1,
@@ -318,13 +332,16 @@
                 acc[m : m + 128, 0:256] += q
                 acc[m : m + 128, 256:384] += kv
 
-    project("own", True)
     gather_q.arrive(1)
     gather_q.send(5)
     gather_q.arrive(2)
     gather_q.send(6)
+    project("own", True)
+    gather_q.leave(5, 6)
     gather_q.arrive(0)
     gather_q.send(3, 4)
+    pltpu.make_async_copy(wo.at[r], wo.at[r], w_recv.at[1]).wait()
+    gather_o.send(0)
     project("m")
     project("p")
     project("x")
@@ -333,14 +350,12 @@
     gather_q.arrive(6)
     gather_q.send(8)
     project("2")
-    pltpu.make_async_copy(wo.at[r], wo.at[r], w_recv.at[1]).wait()
     gather_q.arrive(3)
     gather_q.arrive(4)
     gather_o.send(1, 2)
     project("xm")
     project("xp")
     gather_q.arrive(7, 8)
-    gather_o.send(0)
     project("x2")
 
     is_value_device = lax.rem(t // 2, 2) == 1
@@ -371,6 +386,8 @@
         return carry
 
     lax.fori_loop(1, TP + 1, spread, 0)
+    gather_o.arrive(0)
+    gather_o.send(3, 4)
 
     for copy in cache_copies:
         copy.wait()
@@ -390,7 +407,7 @@
     )
     mixed[Q_ROWS:384, :] = jnp.zeros((384 - Q_ROWS, HD), BF)
 
-    def attend(g, carry):
+    def attend(g):
         gathered = incoming[pl.ds(g * 4, 4)].reshape(512, HD)
         ordered = jnp.dot(pick[...], gathered, preferred_element_type=F32).astype(BF)
         q_g[...] = ordered[0:Q_ROWS]
@@ -422,119 +439,140 @@
             (jnp.concatenate(parts, axis=0) + fresh_part) / total
         ).astype(BF)
         by_head = jnp.dot(unpick[...], mixed[...], preferred_element_type=F32)
-        lanes = pl.multiple_of(g * 1024, 1024)
-        tail_lanes = pl.multiple_of(lax.rem(g, 2) * 1024, 1024)
-        tail_rows = pl.multiple_of(g // 2 * 8, 8)
         heads = [by_head[TOKENS * h : TOKENS * h + TOKENS] for h in range(8)]
-        att[t, :, pl.ds(lanes, 1024)] = jnp.concatenate([x[:MAIN] for x in heads], axis=1).astype(BF)
-        tail_f32[pl.ds(tail_rows, 8), pl.ds(tail_lanes, 1024)] = jnp.concatenate(
-            [x[MAIN:] for x in heads], axis=1
+        last = [x[MAIN:] for x in heads]
+        tail = [jnp.concatenate(pair, axis=0) for pair in zip(last[:4], last[4:])]
+        att[t, g] = jnp.concatenate(
+            [x[:16] for x in heads] + [x[16:MAIN] for x in heads] + tail, axis=1
+        ).astype(BF)
+
+    names = ("own", "m", "p", "x", "2", "xm", "xp", "x2")
+    gathers = [
+        Gather(
+            [lambda block, g=g: att.at[block, g]], [BY_LANES], tp_blocks, tp_neighbours, "pair",
+            ga_send.at[pl.ds(g, 1)], ga_recv.at[pl.ds(g, 1)],
         )
-        return carry
-
-    lax.fori_loop(0, 2, attend, 0)
-    gather_o.arrive(1)
-    gather_o.send(5)
-    gather_o.arrive(2)
-    gather_o.send(6)
-    gather_o.arrive(0)
-    gather_o.send(3, 4)
-    lax.fori_loop(2, KVH, attend, 0)
-    tail[t] = tail_f32[...].astype(BF)
-
-    gather_a = Gather(
-        [att, tail], [BY_ROWS, BY_LANES], tp_blocks, tp_neighbours, ga_send, ga_recv
-    )
-    names = ("own", "m", "p", "x", "2", "xm", "xp", "x2")
-
-    def to_core(i, block, start):
-        for b, buffer in enumerate((att, tail)):
-            copy = pltpu.make_async_remote_copy(
-                src_ref=buffer.at[block], dst_ref=buffer.at[block],
-                send_sem=core_send.at[b, i], recv_sem=core_recv.at[b, i],
-                device_id=(r, core), device_id_type=MESH,
-            )
-            if start == 0:
-                copy.start()
-            elif start == 1:
-                copy.wait_recv()
-            else:
-                copy.wait_send()
-
-    def share(name):
-        to_core(names.index(name), tp_blocks[name], 0)
-
-    gather_a.send(0, 1, 2)
-    share("own")
-    gather_a.arrive(1)
-    gather_a.send(5)
-    gather_a.arrive(2)
-    gather_a.send(6)
-    gather_a.arrive(0)
-    gather_a.send(3, 4)
-    share("m")
-    share("p")
-    share("x")
-    gather_o.arrive(5)
+        for g in range(KVH)
+    ]
+
+    def to_core(g, name, block):
+        i = names.index(name)
+        return pltpu.make_async_remote_copy(
+            src_ref=att.at[block, g], dst_ref=att.at[block, g],
+            send_sem=core_send.at[g, i], recv_sem=core_recv.at[g, i],
+            device_id=(r, core), device_id_type=MESH,
+        )
+
+    def share(g, *group):
+        for name in group:
+            to_core(g, name, tp_blocks[name]).start()
+
+    def first_hop(g):
+        gather = gathers[g]
+        gather.arrive(1)
+        gather.send(5)
+        gather.arrive(2)
+        gather.send(6)
+        gather.arrive(0)
+        gather.send(3, 4)
+        share(g, "m", "p", "x")
+
+    def second_hop(g):
+        gather = gathers[g]
+        gather.arrive(5)
+        gather.send(7)
+        gather.arrive(6)
+        gather.send(8)
+        share(g, "2")
+
+    def third_hop(g):
+        gathers[g].arrive(3)
+        share(g, "xm")
+        gathers[g].arrive(4)
+        share(g, "xp")
+
+    for g in range(KVH):
+        attend(g)
+        gathers[g].send(0, 1, 2)
+        share(g, "own")
+        if g == 1:
+            gather_o.arrive(1)
+            gather_o.send(5)
+            gather_o.arrive(2)
+            gather_o.send(6)
+        if g >= 2:
+            first_hop(g - 2)
+    second_hop(0)
+    first_hop(2)
+    second_hop(1)
+    first_hop(3)
+    gather_o.arrive(3)
     gather_o.send(7)
-    gather_o.arrive(6)
+    gather_o.arrive(4)
     gather_o.send(8)
-    gather_a.arrive(5)
-    gather_a.send(7)
-    gather_a.arrive(6)
-    gather_a.send(8)
-    share("2")
+    second_hop(2)
+    second_hop(3)
 
     chips = {name: tp_blocks[name] // 2 * 2 for name in names}
     flip = 1 - 2 * lax.rem(t, 2)
 
     def from_core(*group):
         for name in group:
-            to_core(names.index(name), tp_blocks[name] + flip, 1)
+            for g in range(KVH):
+                to_core(g, name, tp_blocks[name] + flip).wait_recv()
 
     def output(i, group, chunks):
         for chunk in chunks:
             block = rep_blocks[chunk]
-            lanes = pl.ds(pl.multiple_of(block * 512, 512), 512)
-            tail_lanes = pl.ds(pl.multiple_of(lax.rem(block, 4) * 512, 512), 512)
-            rows = [att[pl.ds(chips[name], 2), :, lanes].reshape(2 * MAIN, 512) for name in group]
-            rows += [
-                tail[pl.ds(chips[name], 2), :, tail_lanes].reshape(4 * TAIL, 512) for name in group
+            g, side = block // 2, lax.rem(block, 2)
+            rows = [
+                att[pl.ds(chips[name], 2), g, :, lanes].reshape(32, 512)
+                for lanes in (
+                    pl.ds(pl.multiple_of(side * 512, 512), 512),
+                    pl.ds(pl.multiple_of(side * 512 + 1024, 512), 512),
+                    pl.ds(2048, 512),
+                )
+                for name in group
             ]
             product = lax.dot_general(
                 jnp.concatenate(rows, axis=0), wo[block], (((1,), (1,)), ((), ())),
                 preferred_element_type=F32,
             )
-            main_out[i] += product[:256]
-            tail_out[i, block // 4] += product[256:]
+            count = 32 * len(group)
+            main_out[i, : 2 * count] += product[: 2 * count]
+            tail_out[i, side, :count] += product[2 * count :]
 
     def store(i, group):
         for n, name in enumerate(group):
             rows = []
-            for s in (2 * n, 2 * n + 1):
-                rows.append(main_out[i, MAIN * s : MAIN * s + MAIN, :])
-                rows.append(
-                    tail_out[i, 0, 16 * s : 16 * s + 8, :]
-                    + tail_out[i, 1, 16 * s + 8 : 16 * s + 16, :]
-                )
-            at = pl.ds(pl.multiple_of(chips[name] * TOKENS, 2 * TOKENS), 2 * TOKENS)
-            out_ref[at, :] = jnp.concatenate(rows, axis=0).astype(BF)
-
-    near, distant = ("own", "m", "p", "x"), ("2", "xm", "xp", "x2")
+            for s in (32 * n, 32 * n + 16):
+                rows.append(main_out[i, s : s + 16, :])
+                rows.append(main_out[i, 32 * len(group) + s : 32 * len(group) + s + 16, :])
+                rows.append(tail_out[i, 0, s : s + 8, :] + tail_out[i, 1, s + 8 : s + 16, :])
+            at = pl.ds(chips[name] * SEQS, 2 * SEQS)
+            out_ref[at] = jnp.concatenate(rows, axis=0).astype(BF).reshape(2 * SEQS, 2, 512)
+
+    near, distant, last = ("own", "m", "p", "x"), ("2", "xm", "xp"), ("x2",)
+    chunks = near + distant + last
     from_core(*near)
-    output(0, near, ("own", "m", "p", "x", "2"))
-    gather_a.arrive(3)
-    share("xm")
-    gather_a.arrive(4)
-    share("xp")
-    gather_o.arrive(3, 4, 7, 8)
-    output(0, near, ("xm", "xp", "x2"))
-    gather_a.arrive(7, 8)
-    share("x2")
+    output(0, near, ("own", "m", "p", "x", "xm", "xp"))
+    for g in range(KVH):
+        third_hop(g)
+    gather_o.arrive(5, 6)
+    output(0, near, ("2",))
+    from_core(*distant)
+    output(1, distant, chunks[:-1])
+    for g in range(KVH):
+        gathers[g].arrive(7, 8)
+        share(g, "x2")
+    gather_o.arrive(7, 8)
+    output(0, near, last)
     store(0, near)
-    from_core(*distant)
-    output(1, distant, ("own", "m", "p", "x") + distant)
+    output(1, distant, last)
     store(1, distant)
+    from_core(*last)
+    output(2, last, chunks)
+    store(2, last)
 
     def sent_q(k, carry):
         dst = lax.rem(t + k, TP)
@@ -565,9 +603,10 @@
     lax.fori_loop(0, REP, delivered_o, 0)
     gather_q.finish()
     gather_o.finish()
-    gather_a.finish()
-    for i, name in enumerate(names):
-        to_core(i, tp_blocks[name], 2)
+    for g in range(KVH):
+        gathers[g].finish()
+        for name in names:
+            to_core(g, name, tp_blocks[name]).wait_send()
 
 
 def body(
@@ -579,7 +618,7 @@
     dma = pltpu.SemaphoreType.DMA
     result = pl.pallas_call(
         kernel,
-        out_shape=jax.ShapeDtypeStruct((ALL_ROWS, 512), BF),
+        out_shape=jax.ShapeDtypeStruct((TP * SEQS, 2, 512), BF),
         in_specs=[vmem, vmem, vmem, hbm, vmem, vmem, hbm, vmem, hbm, hbm, vmem],
         out_specs=vmem,
         scratch_shapes=[
@@ -595,9 +634,7 @@
             pltpu.VMEM((SEQS, KVH, LMAX, HD), BF),
             pltpu.VMEM((TP, 128, HD), BF),
             pltpu.VMEM((TP, 128, HD), BF),
-            pltpu.VMEM((TP, MAIN, HQ * HD), BF),
-            pltpu.VMEM((TP, 2 * TAIL, HQ * HD // 2), BF),
-            pltpu.VMEM((2 * TAIL, HQ * HD // 2), F32),
+            pltpu.VMEM((TP, KVH, 16, 2560), BF),
             pltpu.VMEM((ALL_ROWS, 384), F32),
             pltpu.VMEM((ALL_ROWS, HD), F32),
             pltpu.VMEM((ALL_ROWS, HD), F32),
@@ -607,11 +644,11 @@
             pltpu.VMEM((Q_ROWS, LMAX), F32),
             pltpu.VMEM((Q_ROWS, LMAX), BF),
             pltpu.VMEM((384, HD), BF),
-            pltpu.VMEM((2, 256, 512), F32),
-            pltpu.VMEM((2, 2, 128, 512), F32),
+            pltpu.VMEM((3, 256, 512), F32),
+            pltpu.VMEM((3, 2, 128, 512), F32),
             dma((2,)), dma((2,)), dma((2,)), dma((2,)), dma((2,)), dma((2,)), dma, dma,
-            dma((2, 9)), dma((2, 9)), dma((1, 9)), dma((1, 9)), dma((2, 9)), dma((2, 9)),
-            dma((2, 8)), dma((2, 8)),
+            dma((2, 9)), dma((2, 9)), dma((1, 9)), dma((1, 9)), dma((KVH, 9)), dma((KVH, 9)),
+            dma((KVH, 8)), dma((KVH, 8)),
         ],
         compiler_params=pltpu.CompilerParams(
             collective_id=0, has_side_effects=True, vmem_limit_bytes=62 * 2**20
@@ -619,9 +656,9 @@
     )(
         query_weight, key_weight, value_weight, output_weight,
         query_amax.reshape(HQ, HD), key_amax.reshape(KVH, HD),
-        hidden, positions.reshape(1, -1), cache_keys, cache_values, lengths.reshape(1, -1),
-    )
-    return result.reshape(hidden.shape[0], 2, 512)
+        hidden, positions, cache_keys, cache_values, lengths.reshape(1, -1),
+    )
+    return result
 
 
 def solution(mesh):

time: 131 us -> 113 us (0.86)
  Pallas kernels: 127 us -> 110 us
  local copies, waits for them, and re-layouts: 3.87 us -> 2.37 us
    pallas_call x1, Pallas kernels: 127 us -> 110 us  [body(): pl.pallas_call(kernel, out_shape=jax.ShapeDtypeStruct((TP * SEQS, 2, 512)...]
    reshape x2 -> x0, local copies, waits for them, and re-layouts: 3.87 us -> none  [the longest x1 2.63 us: body(): return result.reshape(hidden.shape[0], 2, 512)]
    unnamed x0 -> x1, local copies, waits for them, and re-layouts: none -> 2.37 us
where the time goes in v4:
time: 113 us; the launch traced here: 112 us
  Pallas kernels  110 us (97%)
  local copies, waits for them, and re-layouts  2.37 us (2%)
    pallas_call x1, Pallas kernels, body(): pl.pallas_call(kernel, out_shape=jax.ShapeDtypeStruct((TP * SEQS, 2, 512)...  110 us
    unnamed x1, local copies, waits for them, and re-layouts  2.37 us

profile of v4, /device:TPU:1, one launch (start us, length us, event | category | flops | bytes accessed | tf_op | source)
XLA Modules:
  0.0 112.3 jit_solution(3610420356177764404)
XLA Ops:
  0.0 109.9 %shard_map.109 = bf16[320,2,512]{2,1,0:T(2,128)(2,1)} custom-call(bf16[64,4096]{1,0:T(8,128)(2,1)} %wq_ref.1, bf16[64,512]{1,0:T(8,128)(2,1)} %wk_ref.1, bf16[64,512]{1,0:T(8,128)(2,1)} %wv_ref.1, bf16[64,4096]{1,0:T(8,128)(2,1)} %wo_ref.1, f32[32,128]{1,0:T(8,128)} %bitcast.3, f32[4,128]{1,0:T(4,128)} %bitcast.4, bf16[320,2,8192]{2,1,0:T(2,128)(2,1)} %hid_ref.1, ...), custom_call_target="tpu_custom_call" | custom-call | tf_op jit(solution)/shard_map/pallas_call | solution.py:619
  109.9 2.4 %copy.13 = bf16[320,2,512]{2,1,0:T(2,128)(2,1)} copy(bf16[320,2,512]{2,1,0:T(2,128)(2,1)} %shard_map.109) | data formatting | bytes 1310720

commit v5 on v4

--- a/solution.py
+++ b/solution.py
@@ -49,26 +49,34 @@
     return view.at[:, pl.ds(view.shape[1] // 2, view.shape[1] // 2)]
 
 
-BY_ROWS = (lambda view: view, top_half, bottom_half)
+def top_part(view):
+    return view.at[pl.ds(0, view.shape[0] * 3 // 16)]
+
+
+def bottom_part(view):
+    return view.at[pl.ds(view.shape[0] * 3 // 16, view.shape[0] * 13 // 16)]
+
+
+BY_ROWS = (lambda view: view, top_half, bottom_half, top_part, bottom_part)
 BY_LANES = (lambda view: view, left_half, right_half)
 
 
+FIRST = (("own", 0, "x", "x"), ("own", 0, "p", "m"), ("own", 0, "m", "p"))
+WHOLE = (("x", 0, "p", "xm"), ("x", 0, "m", "xp"))
+LESS = (("x", 4, "p", "xm"), ("x", 4, "m", "xp"))
+HALVES = (("m", 1, "p", "2"), ("p", 2, "m", "2"))
+PAIR = FIRST + WHOLE + HALVES + (("2", 1, "x", "x2"), ("2", 2, "x", "x2"))
+RING = FIRST + WHOLE + HALVES + (("xm", 1, "p", "x2"), ("xp", 2, "m", "x2"))
+BOTH = FIRST + WHOLE + HALVES + (("2", 1, "x", "x2"), ("xp", 2, "m", "x2"))
+MIXED = (
+    FIRST + LESS + HALVES
+    + (("2", 1, "x", "x2"), ("2", 2, "x", "x2"), ("m", 3, "x", "xm"), ("p", 3, "x", "xp"))
+)
+
+
 class Gather:
-    ARRIVES = (
-        ("x", 0), ("m", 0), ("p", 0), ("xm", 0), ("xp", 0),
-        ("2", 1), ("2", 2), ("x2", 1), ("x2", 2),
-    )
-    SENT = (
-        ("own", 0, "x"), ("own", 0, "p"), ("own", 0, "m"), ("x", 0, "p"), ("x", 0, "m"),
-        ("m", 1, "p"), ("p", 2, "m"),
-    )
-    LAST = {
-        "pair": (("2", 1, "x"), ("2", 2, "x")),
-        "ring": (("xm", 1, "p"), ("xp", 2, "m")),
-    }
-
-    def __init__(self, buffers, parts, blocks, neighbours, last, send_sems, recv_sems):
-        self.sent = self.SENT + self.LAST[last]
+    def __init__(self, plan, buffers, parts, blocks, neighbours, send_sems, recv_sems):
+        self.plan = plan
         self.buffers = buffers
         self.parts = parts
         self.blocks = blocks
@@ -78,12 +86,9 @@
         self.left = set()
 
     def copies(self, step, arriving):
-        if arriving:
-            name, part = self.ARRIVES[step]
-            device = self.neighbours["x"]
-        else:
-            name, part, to = self.sent[step]
-            device = self.neighbours[to]
+        name, part, to, there = self.plan[step]
+        name = there if arriving else name
+        device = self.neighbours[to]
         for b, (buffer, parts) in enumerate(zip(self.buffers, self.parts)):
             view = parts[part](buffer(self.blocks[name]))
             yield pltpu.make_async_remote_copy(
@@ -112,16 +117,16 @@
                 copy.wait_send()
 
     def finish(self):
-        self.leave(*(step for step in range(9) if step not in self.left))
+        self.leave(*(step for step in range(len(self.plan)) if step not in self.left))
 
 
 def kernel(
     wq_ref, wk_ref, wv_ref, wo_ref, qa_ref, ka_ref, hid_ref, pos_ref, ck_ref, cv_ref, len_ref,
     out_ref,
-    qf, kvf, wq, kvw, wo_stage, wo, hid, stage, ck, cv, outgoing, incoming, att,
+    qf, qf2, kvf, wq, wq2, kvw, wo_stage, wo, hid, stage, ck, cv, outgoing, outgoing2, incoming, incoming2, att,
     acc, cosine, sine, pick, unpick, q_g, scores, probs, mixed, main_out, tail_out,
     stage_sems, cache_sems, a_send, a_recv, w_send, w_recv, qkv_send, qkv_recv,
-    gq_send, gq_recv, go_send, go_recv, ga_send, ga_recv, core_send, core_recv,
+    gq_send, gq_recv, gr_send, gr_recv, go_send, go_recv, ga_send, ga_recv, core_send, core_recv,
 ):
     r = lax.axis_index("rep")
     t = lax.axis_index("tp")
@@ -136,6 +141,11 @@
         "xp": other + zp, "xm": other + zm, "x2": other + z2,
     }
     rep_neighbours = {"x": (x_rep, t), "p": (base + zp, t), "m": (base + zm, t)}
+    side = lax.rem(t // 2, 2)
+
+    def across(other_side, rep):
+        return jnp.where(other_side != side, lax.rem(rep + 4, 8), rep)
+
     y = t // 4
     low = lax.rem(t, 4)
     far = lax.rem(low + 2, 4)
@@ -155,6 +165,8 @@
         greet((r, lax.rem(t + k, TP)))
     for k in range(1, REP):
         greet((lax.rem(r + k, REP), t))
+    for k in range(8):
+        greet((x_rep, k // 2 * 4 + 2 - side * 2 + k % 2))
 
     def hidden_copy(i, slot):
         return pltpu.make_async_copy(
@@ -174,13 +186,14 @@
         key_peak = jnp.maximum(key_peak, swap_halves(key_peak))
         factors.append(jnp.sqrt(key_peak / query_peak)[0:1, :])
     for dst in range(TP):
-        factor = jnp.concatenate([factors[dst // 4]] * 2, axis=1)
-        qf[dst] = (wq_ref[:, 256 * dst : 256 * dst + 256].astype(F32) * factor).astype(BF)
+        for n, folded in enumerate((qf, qf2)):
+            at = 256 * dst + HD * n
+            folded[dst] = (wq_ref[:, at : at + HD].astype(F32) * factors[dst // 4]).astype(BF)
     for g in range(KVH):
         kvf[g] = (wk_ref[:, HD * g : HD * g + HD].astype(F32) / factors[g]).astype(BF)
         kvf[KVH + g] = wv_ref[:, HD * g : HD * g + HD]
 
-    pl.semaphore_wait(barrier, TP - 1 + REP - 1)
+    pl.semaphore_wait(barrier, TP - 1 + REP - 1 + 8)
 
     def wo_columns(i):
         return wo_ref.at[:, pl.ds(pl.multiple_of(i * 512, 512), 512)]
@@ -188,7 +201,7 @@
     def wo_scatter(k, carry):
         to = lax.rem(r + k, REP)
         pltpu.make_async_remote_copy(
-            src_ref=wo_columns(to), dst_ref=wo_stage.at[r],
+            src_ref=wo_columns(across(lax.rem(r, 2), to)), dst_ref=wo_stage.at[r],
             send_sem=w_send.at[0], recv_sem=w_recv.at[0],
             device_id=(to, t), device_id_type=MESH,
         ).start()
@@ -201,20 +214,31 @@
 
     def deliver(k, carry):
         dst = lax.rem(t + k, TP)
+        rep = across(lax.rem(dst // 2, 2), r)
         pltpu.make_async_remote_copy(
-            src_ref=qf.at[dst], dst_ref=wq.at[r, q_rows],
+            src_ref=qf.at[dst], dst_ref=wq.at[rep, q_rows],
             send_sem=a_send.at[0], recv_sem=a_recv.at[0],
-            device_id=(r, dst), device_id_type=MESH,
+            device_id=(rep, dst), device_id_type=MESH,
         ).start()
 
         @pl.when(lax.rem(dst, 2) == half)
         def _():
             pltpu.make_async_remote_copy(
-                src_ref=kvf.at[lax.rem(dst, 4) // 2 * 4 + dst // 4], dst_ref=kvw.at[r, kv_rows],
+                src_ref=kvf.at[lax.rem(dst, 4) // 2 * 4 + dst // 4], dst_ref=kvw.at[rep, kv_rows],
                 send_sem=a_send.at[1], recv_sem=a_recv.at[1],
-                device_id=(r, dst), device_id_type=MESH,
+                device_id=(rep, dst), device_id_type=MESH,
             ).start()
 
+        return carry
+
+    def deliver_second(k, carry):
+        dst = lax.rem(t + k, TP)
+        rep = across(lax.rem(dst // 2, 2), r)
+        pltpu.make_async_remote_copy(
+            src_ref=qf2.at[dst], dst_ref=wq2.at[rep, q_rows],
+            send_sem=a_send.at[2], recv_sem=a_recv.at[2],
+            device_id=(rep, dst), device_id_type=MESH,
+        ).start()
         return carry
 
     lax.fori_loop(1, TP, deliver, 0)
@@ -227,20 +251,23 @@
             kvf.at[lax.rem(t, 4) // 2 * 4 + t // 4], kvw.at[r, kv_rows], a_recv.at[1]
         ).start()
 
+    lax.fori_loop(1, TP, deliver_second, 0)
+    pltpu.make_async_copy(qf2.at[t], wq2.at[r, q_rows], a_recv.at[2]).start()
     lax.fori_loop(1, REP, wo_scatter, 0)
-    pltpu.make_async_copy(wo_columns(r), wo_stage.at[r], w_recv.at[0]).start()
+    pltpu.make_async_copy(wo_columns(across(lax.rem(r, 2), r)), wo_stage.at[r], w_recv.at[0]).start()
 
     wo_rows = pl.ds(pl.multiple_of(lax.rem(t, 8) * ROWS, ROWS), ROWS)
 
     def wo_deliver(i, carry):
         dst = 2 * i + half
+        rep = across(lax.rem(i, 2), r)
 
         @pl.when(dst != t)
         def _():
             pltpu.make_async_remote_copy(
-                src_ref=wo_stage.at[i], dst_ref=wo.at[r, wo_rows],
+                src_ref=wo_stage.at[i], dst_ref=wo.at[rep, wo_rows],
                 send_sem=w_send.at[1], recv_sem=w_recv.at[1],
-                device_id=(r, dst), device_id_type=MESH,
+                device_id=(rep, dst), device_id_type=MESH,
             ).start()
 
         @pl.when(dst == t)
@@ -257,8 +284,10 @@
     def relayout(i, carry):
         slot = lax.rem(i, 2)
         hidden_copy(i, slot).wait()
-        columns = pl.ds(pl.multiple_of(i * 1024, 1024), 1024)
-        hid[:, columns] = stage[slot].reshape(ALL_ROWS, 1024)
+        block = stage[slot].reshape(ALL_ROWS, 1024)
+        for n in range(8):
+            at = pl.multiple_of(across(n % 2, i) * 1024 + n * 128, 128)
+            hid[:, pl.ds(at, 128)] = block[:, n * 128 : n * 128 + 128]
 
         @pl.when(i < 6)
         def _():
@@ -267,15 +296,23 @@
         return carry
 
     gather_q = Gather(
+        PAIR,
         [lambda block: wq.at[block], lambda block: kvw.at[block]], [BY_ROWS, BY_ROWS], rep_blocks, rep_neighbours,
-        "pair", gq_send, gq_recv,
+        gq_send, gq_recv,
+    )
+    gather_r = Gather(
+        PAIR, [lambda block: wq2.at[block]], [BY_ROWS], rep_blocks, rep_neighbours,
+        gr_send, gr_recv,
     )
     gather_o = Gather(
-        [lambda block: wo.at[block]], [BY_ROWS], rep_blocks, rep_neighbours, "ring", go_send, go_recv,
+        RING,
+        [lambda block: wo.at[block]], [BY_ROWS], rep_blocks, rep_neighbours, go_send, go_recv,
     )
     pltpu.make_async_copy(wq.at[r], wq.at[r], a_recv.at[0]).wait()
     pltpu.make_async_copy(kvw.at[r], kvw.at[r], a_recv.at[1]).wait()
     gather_q.send(0, 1, 2)
+    pltpu.make_async_copy(wq2.at[r], wq2.at[r], a_recv.at[2]).wait()
+    gather_r.send(0, 1, 2)
     pltpu.make_async_copy(wo_stage, wo_stage, w_recv.at[0]).wait()
     lax.fori_loop(0, REP, wo_deliver, 0)
     for copy in cache_copies:
@@ -301,11 +338,14 @@
 
     row, col = iota((576, 512), 0), iota((576, 512), 1)
     b, w = row // 16, lax.rem(row, 16)
-    source = w // 4 * 128 + lax.rem(w, 2) * TOKENS + 2 * b + lax.rem(w // 2, 2)
+    token = 2 * b + lax.rem(w // 2, 2)
+    source = w // 4 * 80 + token
+    source = jnp.where(lax.rem(w, 2) == 0, source, 320 + w // 4 * 48 + token)
     token = lax.rem(row - Q_ROWS + 128, 128)
-    col_row, col_dev = lax.rem(col, 128), col // 128
-    fresh_row = jnp.logical_and(col_row == 80 + token, token < TOKENS)
-    is_key, is_value = row < Q_ROWS + 128, col_dev >= 2
+    fresh_row = jnp.logical_and(
+        jnp.logical_and(col < 320, lax.rem(col, 80) == TOKENS + token), token < TOKENS
+    )
+    is_key, is_value = row < Q_ROWS + 128, col >= 160
     hit = jnp.where(
         row < Q_ROWS, (col == source).astype(F32),
         jnp.logical_and(fresh_row, is_key != is_value).astype(F32),
@@ -326,22 +366,74 @@
             q = jnp.dot(hid[m : m + 128, pl.ds(q_at, 1024)], wq[block], preferred_element_type=F32)
             kv = jnp.dot(hid[m : m + 128, pl.ds(kv_at, 512)], kvw[block], preferred_element_type=F32)
             if first:
-                acc[m : m + 128, 0:256] = q
+                acc[m : m + 128, 0:128] = q
                 acc[m : m + 128, 256:384] = kv
             else:
-                acc[m : m + 128, 0:256] += q
+                acc[m : m + 128, 0:128] += q
                 acc[m : m + 128, 256:384] += kv
+
+    def project_second(name, first=False):
+        block = rep_blocks[name]
+        q_at = pl.multiple_of(block * 1024, 1024)
+        for m in range(0, ALL_ROWS, 128):
+            q = jnp.dot(hid[m : m + 128, pl.ds(q_at, 1024)], wq2[block], preferred_element_type=F32)
+            if first:
+                acc[m : m + 128, 128:256] = q
+            else:
+                acc[m : m + 128, 128:256] += q
+
+    is_value_device = lax.rem(t // 2, 2) == 1
+
+    def rotate(x, rows):
+        return x * cosine[rows, :] + swap_halves(x) * sine[rows, :]
+
+    def to_owner(buffer, landing, i, k):
+        dst = lax.rem(t + k, TP)
+
+        @pl.when(k < TP)
+        def _():
+            pltpu.make_async_remote_copy(
+                src_ref=buffer.at[dst], dst_ref=landing.at[t],
+                send_sem=qkv_send.at[i], recv_sem=qkv_recv.at[i],
+                device_id=(r, dst), device_id_type=MESH,
+            ).start()
+
+        @pl.when(k == TP)
+        def _():
+            pltpu.make_async_copy(buffer.at[dst], landing.at[t], qkv_recv.at[i]).start()
+
+    def spread(k, carry):
+        dst = lax.rem(t + k, TP)
+        rows = pl.ds(pl.multiple_of(dst * TOKENS, 8), TOKENS)
+        kv = acc[rows, 256:384]
+        kv = jnp.where(is_value_device, kv, rotate(kv, rows))
+        outgoing[dst] = jnp.concatenate([rotate(acc[rows, 0:128], rows), kv], axis=0).astype(BF)
+        to_owner(outgoing, incoming, 0, k)
+        return carry
+
+    def spread_second(k, carry):
+        dst = lax.rem(t + k, TP)
+        rows = pl.ds(pl.multiple_of(dst * TOKENS, 8), TOKENS)
+        q = rotate(acc[rows, 128:256], rows)
+        outgoing2[dst] = jnp.concatenate([q, jnp.zeros((8, HD), F32)], axis=0).astype(BF)
+        to_owner(outgoing2, incoming2, 1, k)
+        return carry
 
     gather_q.arrive(1)
     gather_q.send(5)
     gather_q.arrive(2)
     gather_q.send(6)
     project("own", True)
+    project_second("own", True)
     gather_q.leave(5, 6)
     gather_q.arrive(0)
     gather_q.send(3, 4)
-    pltpu.make_async_copy(wo.at[r], wo.at[r], w_recv.at[1]).wait()
-    gather_o.send(0)
+    gather_r.arrive(1)
+    gather_r.send(5)
+    gather_r.arrive(2)
+    gather_r.send(6)
+    gather_r.arrive(0)
+    gather_r.send(3, 4)
     project("m")
     project("p")
     project("x")
@@ -350,48 +442,38 @@
     gather_q.arrive(6)
     gather_q.send(8)
     project("2")
+    pltpu.make_async_copy(wo.at[r], wo.at[r], w_recv.at[1]).wait()
+    gather_o.send(0)
+    project_second("m")
+    project_second("p")
+    project_second("x")
+    gather_r.arrive(5)
+    gather_r.send(7)
+    gather_r.arrive(6)
+    gather_r.send(8)
     gather_q.arrive(3)
+    project("xm")
     gather_q.arrive(4)
-    gather_o.send(1, 2)
-    project("xm")
     project("xp")
     gather_q.arrive(7, 8)
     project("x2")
-
-    is_value_device = lax.rem(t // 2, 2) == 1
-
-    def spread(k, carry):
-        dst = lax.rem(t + k, TP)
-        rows = pl.ds(pl.multiple_of(dst * TOKENS, 8), TOKENS)
-        c, s = cosine[rows, :], sine[rows, :]
-        q0, q1, kv = acc[rows, 0:128], acc[rows, 128:256], acc[rows, 256:384]
-        q0 = q0 * c + swap_halves(q0) * s
-        q1 = q1 * c + swap_halves(q1) * s
-        kv = jnp.where(is_value_device, kv, kv * c + swap_halves(kv) * s)
-        packed = jnp.concatenate([q0, q1, kv, jnp.zeros((8, HD), F32)], axis=0).astype(BF)
-        outgoing[dst] = packed
-
-        @pl.when(k < TP)
-        def _():
-            pltpu.make_async_remote_copy(
-                src_ref=outgoing.at[dst], dst_ref=incoming.at[t],
-                send_sem=qkv_send, recv_sem=qkv_recv,
-                device_id=(r, dst), device_id_type=MESH,
-            ).start()
-
-        @pl.when(k == TP)
-        def _():
-            pltpu.make_async_copy(outgoing.at[dst], incoming.at[t], qkv_recv).start()
-
-        return carry
-
     lax.fori_loop(1, TP + 1, spread, 0)
+    project_second("2")
+    gather_r.arrive(3)
+    gather_r.arrive(4)
+    gather_o.send(1, 2)
+    project_second("xm")
+    project_second("xp")
+    gather_r.arrive(7, 8)
+    project_second("x2")
+    lax.fori_loop(1, TP + 1, spread_second, 0)
     gather_o.arrive(0)
     gather_o.send(3, 4)
 
     for copy in cache_copies:
         copy.wait()
-    pltpu.make_async_copy(incoming, incoming, qkv_recv).wait()
+    pltpu.make_async_copy(incoming, incoming, qkv_recv.at[0]).wait()
+    pltpu.make_async_copy(incoming2, incoming2, qkv_recv.at[1]).wait()
 
     lengths = jnp.sum(
         jnp.where(
@@ -408,7 +490,13 @@
     mixed[Q_ROWS:384, :] = jnp.zeros((384 - Q_ROWS, HD), BF)
 
     def attend(g):
-        gathered = incoming[pl.ds(g * 4, 4)].reshape(512, HD)
+        gathered = jnp.concatenate(
+            [
+                incoming[pl.ds(g * 4, 4)].reshape(8 * TOKENS, HD),
+                incoming2[pl.ds(g * 4, 4)].reshape(192, HD),
+            ],
+            axis=0,
+        )
         ordered = jnp.dot(pick[...], gathered, preferred_element_type=F32).astype(BF)
         q_g[...] = ordered[0:Q_ROWS]
         key_new, value_new = ordered[Q_ROWS : Q_ROWS + 128], ordered[Q_ROWS + 128 :]
@@ -449,7 +537,8 @@
     names = ("own", "m", "p", "x", "2", "xm", "xp", "x2")
     gathers = [
         Gather(
-            [lambda block, g=g: att.at[block, g]], [BY_LANES], tp_blocks, tp_neighbours, "pair",
+            PAIR,
+            [lambda block, g=g: att.at[block, g]], [BY_LANES], tp_blocks, tp_neighbours,
             ga_send.at[pl.ds(g, 1)], ga_recv.at[pl.ds(g, 1)],
         )
         for g in range(KVH)
@@ -495,21 +584,21 @@
         attend(g)
         gathers[g].send(0, 1, 2)
         share(g, "own")
-        if g == 1:
+        if g == 0:
             gather_o.arrive(1)
             gather_o.send(5)
             gather_o.arrive(2)
             gather_o.send(6)
         if g >= 2:
             first_hop(g - 2)
+    gather_o.arrive(3)
+    gather_o.send(7)
+    gather_o.arrive(4)
+    gather_o.send(8)
     second_hop(0)
     first_hop(2)
     second_hop(1)
     first_hop(3)
-    gather_o.arrive(3)
-    gather_o.send(7)
-    gather_o.arrive(4)
-    gather_o.send(8)
     second_hop(2)
     second_hop(3)
 
@@ -577,7 +666,9 @@
     def sent_q(k, carry):
         dst = lax.rem(t + k, TP)
         pltpu.make_async_copy(qf.at[dst], qf.at[dst], a_send.at[0]).wait()
-        pltpu.make_async_copy(outgoing.at[dst], outgoing.at[dst], qkv_send).wait()
+        pltpu.make_async_copy(qf2.at[dst], qf2.at[dst], a_send.at[2]).wait()
+        pltpu.make_async_copy(outgoing.at[dst], outgoing.at[dst], qkv_send.at[0]).wait()
+        pltpu.make_async_copy(outgoing2.at[dst], outgoing2.at[dst], qkv_send.at[1]).wait()
 
         @pl.when(lax.rem(dst, 2) == half)
         def _():
@@ -602,6 +693,7 @@
 
     lax.fori_loop(0, REP, delivered_o, 0)
     gather_q.finish()
+    gather_r.finish()
     gather_o.finish()
     for g in range(KVH):
         gathers[g].finish()
@@ -622,9 +714,11 @@
         in_specs=[vmem, vmem, vmem, hbm, vmem, vmem, hbm, vmem, hbm, hbm, vmem],
         out_specs=vmem,
         scratch_shapes=[
-            pltpu.VMEM((TP, ROWS, 256), BF),
+            pltpu.VMEM((TP, ROWS, HD), BF),
+            pltpu.VMEM((TP, ROWS, HD), BF),
             pltpu.VMEM((2 * KVH, ROWS, HD), BF),
-            pltpu.VMEM((REP, TP * ROWS, 256), BF),
+            pltpu.VMEM((REP, TP * ROWS, HD), BF),
+            pltpu.VMEM((REP, TP * ROWS, HD), BF),
             pltpu.VMEM((REP, 8 * ROWS, HD), BF),
             pltpu.VMEM((REP, ROWS, 512), BF),
             pltpu.VMEM((REP, 512, 512), BF),
@@ -632,8 +726,10 @@
             pltpu.VMEM((2, 320, 2, 1024), BF),
             pltpu.VMEM((SEQS, KVH, LMAX, HD), BF),
             pltpu.VMEM((SEQS, KVH, LMAX, HD), BF),
-            pltpu.VMEM((TP, 128, HD), BF),
-            pltpu.VMEM((TP, 128, HD), BF),
+            pltpu.VMEM((TP, 80, HD), BF),
+            pltpu.VMEM((TP, 48, HD), BF),
+            pltpu.VMEM((TP, 80, HD), BF),
+            pltpu.VMEM((TP, 48, HD), BF),
             pltpu.VMEM((TP, KVH, 16, 2560), BF),
             pltpu.VMEM((ALL_ROWS, 384), F32),
             pltpu.VMEM((ALL_ROWS, HD), F32),
@@ -646,8 +742,8 @@
             pltpu.VMEM((384, HD), BF),
             pltpu.VMEM((3, 256, 512), F32),
             pltpu.VMEM((3, 2, 128, 512), F32),
-            dma((2,)), dma((2,)), dma((2,)), dma((2,)), dma((2,)), dma((2,)), dma, dma,
-            dma((2, 9)), dma((2, 9)), dma((1, 9)), dma((1, 9)), dma((KVH, 9)), dma((KVH, 9)),
+            dma((2,)), dma((2,)), dma((3,)), dma((3,)), dma((2,)), dma((2,)), dma((2,)), dma((2,)),
+            dma((2, 11)), dma((2, 11)), dma((1, 9)), dma((1, 9)), dma((1, 9)), dma((1, 9)), dma((KVH, 9)), dma((KVH, 9)),
             dma((KVH, 8)), dma((KVH, 8)),
         ],
         compiler_params=pltpu.CompilerParams(

time: 113 us -> 106 us (0.938)
  Pallas kernels: 110 us -> 103 us
    pallas_call x1, Pallas kernels: 110 us -> 103 us  [body(): pl.pallas_call(kernel, out_shape=jax.ShapeDtypeStruct((TP * SEQS, 2, 512)...]
where the time goes in v5:
time: 106 us; the launch traced here: 105 us
  Pallas kernels  103 us (97%)
  local copies, waits for them, and re-layouts  2.37 us (2%)
    pallas_call x1, Pallas kernels, body(): pl.pallas_call(kernel, out_shape=jax.ShapeDtypeStruct((TP * SEQS, 2, 512)...  103 us
    unnamed x1, local copies, waits for them, and re-layouts  2.37 us

profile of v5, /device:TPU:1, one launch (start us, length us, event | category | flops | bytes accessed | tf_op | source)
XLA Modules:
  0.0 105.4 jit_solution(15880429020919287822)
XLA Ops:
  0.0 103.0 %shard_map.109 = bf16[320,2,512]{2,1,0:T(2,128)(2,1)} custom-call(bf16[64,4096]{1,0:T(8,128)(2,1)} %wq_ref.1, bf16[64,512]{1,0:T(8,128)(2,1)} %wk_ref.1, bf16[64,512]{1,0:T(8,128)(2,1)} %wv_ref.1, bf16[64,4096]{1,0:T(8,128)(2,1)} %wo_ref.1, f32[32,128]{1,0:T(8,128)} %bitcast.3, f32[4,128]{1,0:T(4,128)} %bitcast.4, bf16[320,2,8192]{2,1,0:T(2,128)(2,1)} %hid_ref.1, ...), custom_call_target="tpu_custom_call" | custom-call | tf_op jit(solution)/shard_map/pallas_call | solution.py:711
  103.0 2.4 %copy.13 = bf16[320,2,512]{2,1,0:T(2,128)(2,1)} copy(bf16[320,2,512]{2,1,0:T(2,128)(2,1)} %shard_map.109) | data formatting | bytes 1310720

commit v6 on v5

--- a/solution.py
+++ b/solution.py
@@ -18,7 +18,7 @@
 ALL_ROWS = TP * TOKENS
 MAIN = 32
 TAIL = TOKENS - MAIN
-Q_ROWS = SEQS * 16
+H_ROWS = SEQS * 8
 ROPE_THETA = 1000000.0
 MESH = pl.DeviceIdType.MESH
 BF = jnp.bfloat16
@@ -49,29 +49,16 @@
     return view.at[:, pl.ds(view.shape[1] // 2, view.shape[1] // 2)]
 
 
-def top_part(view):
-    return view.at[pl.ds(0, view.shape[0] * 3 // 16)]
-
-
-def bottom_part(view):
-    return view.at[pl.ds(view.shape[0] * 3 // 16, view.shape[0] * 13 // 16)]
-
-
-BY_ROWS = (lambda view: view, top_half, bottom_half, top_part, bottom_part)
+BY_ROWS = (lambda view: view, top_half, bottom_half)
 BY_LANES = (lambda view: view, left_half, right_half)
 
 
 FIRST = (("own", 0, "x", "x"), ("own", 0, "p", "m"), ("own", 0, "m", "p"))
 WHOLE = (("x", 0, "p", "xm"), ("x", 0, "m", "xp"))
-LESS = (("x", 4, "p", "xm"), ("x", 4, "m", "xp"))
 HALVES = (("m", 1, "p", "2"), ("p", 2, "m", "2"))
 PAIR = FIRST + WHOLE + HALVES + (("2", 1, "x", "x2"), ("2", 2, "x", "x2"))
 RING = FIRST + WHOLE + HALVES + (("xm", 1, "p", "x2"), ("xp", 2, "m", "x2"))
 BOTH = FIRST + WHOLE + HALVES + (("2", 1, "x", "x2"), ("xp", 2, "m", "x2"))
-MIXED = (
-    FIRST + LESS + HALVES
-    + (("2", 1, "x", "x2"), ("2", 2, "x", "x2"), ("m", 3, "x", "xm"), ("p", 3, "x", "xp"))
-)
 
 
 class Gather:
@@ -124,7 +111,7 @@
     wq_ref, wk_ref, wv_ref, wo_ref, qa_ref, ka_ref, hid_ref, pos_ref, ck_ref, cv_ref, len_ref,
     out_ref,
     qf, qf2, kvf, wq, wq2, kvw, wo_stage, wo, hid, stage, ck, cv, outgoing, outgoing2, incoming, incoming2, att,
-    acc, cosine, sine, pick, unpick, q_g, scores, probs, mixed, main_out, tail_out,
+    acc, cosine, sine, pick, pick2, unpick, fresh_kv, scores, probs, mixed, main_out, tail_out,
     stage_sems, cache_sems, a_send, a_recv, w_send, w_recv, qkv_send, qkv_recv,
     gq_send, gq_recv, gr_send, gr_recv, go_send, go_recv, ga_send, ga_recv, core_send, core_recv,
 ):
@@ -301,7 +288,7 @@
         gq_send, gq_recv,
     )
     gather_r = Gather(
-        PAIR, [lambda block: wq2.at[block]], [BY_ROWS], rep_blocks, rep_neighbours,
+        BOTH, [lambda block: wq2.at[block]], [BY_ROWS], rep_blocks, rep_neighbours,
         gr_send, gr_recv,
     )
     gather_o = Gather(
@@ -336,24 +323,22 @@
     main_out[...] = jnp.zeros_like(main_out)
     tail_out[...] = jnp.zeros_like(tail_out)
 
-    row, col = iota((576, 512), 0), iota((576, 512), 1)
-    b, w = row // 16, lax.rem(row, 16)
-    token = 2 * b + lax.rem(w // 2, 2)
-    source = w // 4 * 80 + token
-    source = jnp.where(lax.rem(w, 2) == 0, source, 320 + w // 4 * 48 + token)
-    token = lax.rem(row - Q_ROWS + 128, 128)
-    fresh_row = jnp.logical_and(
-        jnp.logical_and(col < 320, lax.rem(col, 80) == TOKENS + token), token < TOKENS
-    )
-    is_key, is_value = row < Q_ROWS + 128, col >= 160
+    row, col = iota((416, 320), 0), iota((416, 320), 1)
+    order, token = row // 8, lax.rem(row - H_ROWS + 256, 128)
+    source = lax.rem(row, 8) // 2 * 80 + 2 * order + lax.rem(row, 2)
+    fresh_row = jnp.logical_and(lax.rem(col, 80) == TOKENS + token, token < TOKENS)
+    is_key, is_value = row < H_ROWS + 128, col >= 160
     hit = jnp.where(
-        row < Q_ROWS, (col == source).astype(F32),
+        row < H_ROWS, (col == source).astype(F32),
         jnp.logical_and(fresh_row, is_key != is_value).astype(F32),
     )
     pick[...] = hit.astype(BF)
-    row, col = iota((Q_ROWS, 384), 0), iota((Q_ROWS, 384), 1)
+    row, col = iota((H_ROWS, 192), 0), iota((H_ROWS, 192), 1)
+    source = lax.rem(row, 8) // 2 * 48 + row // 8 * 2 + lax.rem(row, 2)
+    pick2[...] = (col == source).astype(F32).astype(BF)
+    row, col = iota((H_ROWS, 256), 0), iota((H_ROWS, 256), 1)
     head, token = row // TOKENS, lax.rem(row, TOKENS)
-    source = token // 2 * 16 + head // 2 * 4 + lax.rem(token, 2) * 2 + lax.rem(head, 2)
+    source = token // 2 * 8 + head * 2 + lax.rem(token, 2)
     unpick[...] = (col == source).astype(F32).astype(BF)
 
     kv_half = lax.rem(t, 2) * 512
@@ -450,7 +435,6 @@
     gather_r.arrive(5)
     gather_r.send(7)
     gather_r.arrive(6)
-    gather_r.send(8)
     gather_q.arrive(3)
     project("xm")
     gather_q.arrive(4)
@@ -461,6 +445,7 @@
     project_second("2")
     gather_r.arrive(3)
     gather_r.arrive(4)
+    gather_r.send(8)
     gather_o.send(1, 2)
     project_second("xm")
     project_second("xp")
@@ -472,43 +457,37 @@
 
     for copy in cache_copies:
         copy.wait()
-    pltpu.make_async_copy(incoming, incoming, qkv_recv.at[0]).wait()
-    pltpu.make_async_copy(incoming2, incoming2, qkv_recv.at[1]).wait()
-
     lengths = jnp.sum(
         jnp.where(
-            iota((Q_ROWS, SEQS), 0) // 16 == iota((Q_ROWS, SEQS), 1), len_ref[...].astype(F32), 0.0
+            iota((H_ROWS, SEQS), 0) // 8 == iota((H_ROWS, SEQS), 1), len_ref[...].astype(F32), 0.0
         ),
         axis=1,
         keepdims=True,
     )
-    live = iota((Q_ROWS, LMAX), 1).astype(F32) < lengths
-    row, col = iota((Q_ROWS, 128), 0), iota((Q_ROWS, 128), 1)
-    fresh_live = jnp.logical_and(
-        row // 16 == col // 2, lax.rem(col, 2) <= lax.rem(lax.rem(row, 16) // 2, 2)
-    )
-    mixed[Q_ROWS:384, :] = jnp.zeros((384 - Q_ROWS, HD), BF)
-
-    def attend(g):
-        gathered = jnp.concatenate(
-            [
-                incoming[pl.ds(g * 4, 4)].reshape(8 * TOKENS, HD),
-                incoming2[pl.ds(g * 4, 4)].reshape(192, HD),
-            ],
-            axis=0,
-        )
-        ordered = jnp.dot(pick[...], gathered, preferred_element_type=F32).astype(BF)
-        q_g[...] = ordered[0:Q_ROWS]
-        key_new, value_new = ordered[Q_ROWS : Q_ROWS + 128], ordered[Q_ROWS + 128 :]
+    live = iota((H_ROWS, LMAX), 1).astype(F32) < lengths
+    row, col = iota((H_ROWS, 128), 0), iota((H_ROWS, 128), 1)
+    fresh_live = jnp.logical_and(row // 8 == col // 2, lax.rem(col, 2) <= lax.rem(row, 2))
+    mixed[H_ROWS:256, :] = jnp.zeros((256 - H_ROWS, HD), BF)
+
+    def attend(part, g):
+        if part == 0:
+            gathered = incoming[pl.ds(g * 4, 4)].reshape(320, HD)
+            ordered = jnp.dot(pick[...], gathered, preferred_element_type=F32)
+            fresh_kv[g] = ordered[H_ROWS:].astype(BF)
+            ordered = ordered[:H_ROWS]
+        else:
+            gathered = incoming2[pl.ds(g * 4, 4)].reshape(192, HD)
+            ordered = jnp.dot(pick2[...], gathered, preferred_element_type=F32)
+        key_new, value_new = fresh_kv[g, 0:128], fresh_kv[g, 128:256]
         for b in range(SEQS):
-            scores[16 * b : 16 * b + 16, :] = lax.dot_general(
-                q_g[16 * b : 16 * b + 16, :], ck[b, g], (((1,), (1,)), ((), ())),
+            scores[8 * b : 8 * b + 8, :] = lax.dot_general(
+                ordered[8 * b : 8 * b + 8].astype(BF), ck[b, g], (((1,), (1,)), ((), ())),
                 preferred_element_type=F32,
             )
         scale = HD ** (-0.5)
         cached = jnp.where(live, scores[...] * scale, -jnp.inf)
         fresh = lax.dot_general(
-            q_g[...], key_new, (((1,), (1,)), ((), ())), preferred_element_type=F32
+            ordered.astype(BF), key_new, (((1,), (1,)), ((), ())), preferred_element_type=F32
         )
         fresh = jnp.where(fresh_live, fresh * scale, -jnp.inf)
         top = jnp.maximum(
@@ -517,20 +496,19 @@
         cached = jnp.exp(cached - top)
         fresh = jnp.exp(fresh - top)
         total = jnp.sum(cached, axis=1, keepdims=True) + jnp.sum(fresh, axis=1, keepdims=True)
-        probs[...] = cached.astype(BF)
+        probs[...] = cached
         fresh_part = jnp.dot(fresh.astype(BF), value_new, preferred_element_type=F32)
         parts = [
-            jnp.dot(probs[16 * b : 16 * b + 16, :], cv[b, g], preferred_element_type=F32)
+            jnp.dot(probs[8 * b : 8 * b + 8, :].astype(BF), cv[b, g], preferred_element_type=F32)
             for b in range(SEQS)
         ]
-        mixed[0:Q_ROWS, :] = (
-            (jnp.concatenate(parts, axis=0) + fresh_part) / total
-        ).astype(BF)
+        mixed[0:H_ROWS, :] = ((jnp.concatenate(parts, axis=0) + fresh_part) / total).astype(BF)
         by_head = jnp.dot(unpick[...], mixed[...], preferred_element_type=F32)
-        heads = [by_head[TOKENS * h : TOKENS * h + TOKENS] for h in range(8)]
+        heads = [by_head[TOKENS * h : TOKENS * h + TOKENS] for h in range(4)]
         last = [x[MAIN:] for x in heads]
-        tail = [jnp.concatenate(pair, axis=0) for pair in zip(last[:4], last[4:])]
-        att[t, g] = jnp.concatenate(
+        tail = [jnp.concatenate(pair, axis=0) for pair in zip(last[:2], last[2:])]
+        at = g % 2 * 1280
+        att[t, part * 2 + g // 2, :, at : at + 1280] = jnp.concatenate(
             [x[:16] for x in heads] + [x[16:MAIN] for x in heads] + tail, axis=1
         ).astype(BF)
 
@@ -580,24 +558,33 @@
         gathers[g].arrive(4)
         share(g, "xp")
 
-    for g in range(KVH):
-        attend(g)
-        gathers[g].send(0, 1, 2)
-        share(g, "own")
-        if g == 0:
-            gather_o.arrive(1)
-            gather_o.send(5)
-            gather_o.arrive(2)
-            gather_o.send(6)
-        if g >= 2:
-            first_hop(g - 2)
+    pltpu.make_async_copy(incoming, incoming, qkv_recv.at[0]).wait()
+
+    def attend_pair(piece):
+        part, first = piece // 2, piece % 2 * 2
+        attend(part, first)
+        attend(part, first + 1)
+        gathers[piece].send(0, 1, 2)
+        share(piece, "own")
+
+    attend_pair(0)
+    gather_o.arrive(1)
+    gather_o.send(5)
+    gather_o.arrive(2)
+    gather_o.send(6)
+    attend_pair(1)
+    first_hop(0)
+    pltpu.make_async_copy(incoming2, incoming2, qkv_recv.at[1]).wait()
+    attend_pair(2)
+    first_hop(1)
+    second_hop(0)
+    attend_pair(3)
+    first_hop(2)
+    second_hop(1)
     gather_o.arrive(3)
     gather_o.send(7)
     gather_o.arrive(4)
     gather_o.send(8)
-    second_hop(0)
-    first_hop(2)
-    second_hop(1)
     first_hop(3)
     second_hop(2)
     second_hop(3)
@@ -614,13 +601,20 @@
         for chunk in chunks:
             block = rep_blocks[chunk]
             g, side = block // 2, lax.rem(block, 2)
+            base = lax.rem(g, 2) * 1280
             rows = [
-                att[pl.ds(chips[name], 2), g, :, lanes].reshape(32, 512)
-                for lanes in (
-                    pl.ds(pl.multiple_of(side * 512, 512), 512),
-                    pl.ds(pl.multiple_of(side * 512 + 1024, 512), 512),
-                    pl.ds(2048, 512),
+                jnp.concatenate(
+                    [
+                        att[
+                            pl.ds(chips[name], 2), part * 2 + g // 2, :,
+                            pl.ds(pl.multiple_of(base + at + n * 128, 128), 128),
+                        ].reshape(32, 128)
+                        for n in range(2)
+                        for part in range(2)
+                    ],
+                    axis=1,
                 )
+                for at in (side * 256, side * 256 + 512, 1024)
                 for name in group
             ]
             product = lax.dot_general(
@@ -654,14 +648,12 @@
     for g in range(KVH):
         gathers[g].arrive(7, 8)
         share(g, "x2")
+    from_core(*last)
+    output(2, last, chunks[:-1])
     gather_o.arrive(7, 8)
-    output(0, near, last)
-    store(0, near)
-    output(1, distant, last)
-    store(1, distant)
-    from_core(*last)
-    output(2, last, chunks)
-    store(2, last)
+    for i, group in enumerate((near, distant, last)):
+        output(i, group, last)
+        store(i, group)
 
     def sent_q(k, carry):
         dst = lax.rem(t + k, TP)
@@ -734,16 +726,17 @@
             pltpu.VMEM((ALL_ROWS, 384), F32),
             pltpu.VMEM((ALL_ROWS, HD), F32),
             pltpu.VMEM((ALL_ROWS, HD), F32),
-            pltpu.VMEM((576, 512), BF),
-            pltpu.VMEM((Q_ROWS, 384), BF),
-            pltpu.VMEM((Q_ROWS, HD), BF),
-            pltpu.VMEM((Q_ROWS, LMAX), F32),
-            pltpu.VMEM((Q_ROWS, LMAX), BF),
-            pltpu.VMEM((384, HD), BF),
+            pltpu.VMEM((416, 320), BF),
+            pltpu.VMEM((H_ROWS, 192), BF),
+            pltpu.VMEM((H_ROWS, 256), BF),
+            pltpu.VMEM((KVH, 256, HD), BF),
+            pltpu.VMEM((H_ROWS, LMAX), F32),
+            pltpu.VMEM((H_ROWS, LMAX), F32),
+            pltpu.VMEM((256, HD), BF),
             pltpu.VMEM((3, 256, 512), F32),
             pltpu.VMEM((3, 2, 128, 512), F32),
             dma((2,)), dma((2,)), dma((3,)), dma((3,)), dma((2,)), dma((2,)), dma((2,)), dma((2,)),
-            dma((2, 11)), dma((2, 11)), dma((1, 9)), dma((1, 9)), dma((1, 9)), dma((1, 9)), dma((KVH, 9)), dma((KVH, 9)),
+            dma((2, 9)), dma((2, 9)), dma((1, 9)), dma((1, 9)), dma((1, 9)), dma((1, 9)), dma((KVH, 9)), dma((KVH, 9)),
             dma((KVH, 8)), dma((KVH, 8)),
         ],
         compiler_params=pltpu.CompilerParams(

time: 106 us -> 104 us (0.981)
  Pallas kernels: 103 us -> 101 us
    pallas_call x1, Pallas kernels: 103 us -> 101 us  [body(): pl.pallas_call(kernel, out_shape=jax.ShapeDtypeStruct((TP * SEQS, 2, 512)...]
where the time goes in v6:
time: 104 us; the launch traced here: 103 us
  Pallas kernels  101 us (97%)
  local copies, waits for them, and re-layouts  2.37 us (2%)
    pallas_call x1, Pallas kernels, body(): pl.pallas_call(kernel, out_shape=jax.ShapeDtypeStruct((TP * SEQS, 2, 512)...  101 us
    unnamed x1, local copies, waits for them, and re-layouts  2.37 us

profile of v6, /device:TPU:1, one launch (start us, length us, event | category | flops | bytes accessed | tf_op | source)
XLA Modules:
  0.0 103.5 jit_solution(10556666878254717353)
XLA Ops:
  0.0 101.1 %shard_map.109 = bf16[320,2,512]{2,1,0:T(2,128)(2,1)} custom-call(bf16[64,4096]{1,0:T(8,128)(2,1)} %wq_ref.1, bf16[64,512]{1,0:T(8,128)(2,1)} %wk_ref.1, bf16[64,512]{1,0:T(8,128)(2,1)} %wv_ref.1, bf16[64,4096]{1,0:T(8,128)(2,1)} %wo_ref.1, f32[32,128]{1,0:T(8,128)} %bitcast.3, f32[4,128]{1,0:T(4,128)} %bitcast.4, bf16[320,2,8192]{2,1,0:T(2,128)(2,1)} %hid_ref.1, ...), custom_call_target="tpu_custom_call" | custom-call | tf_op jit(solution)/shard_map/pallas_call | solution.py:703
  101.1 2.4 %copy.13 = bf16[320,2,512]{2,1,0:T(2,128)(2,1)} copy(bf16[320,2,512]{2,1,0:T(2,128)(2,1)} %shard_map.109) | data formatting | bytes 1310720
